TPU v7x, 32 devices: a whole 2x2x4 slice. The times are simulated.
32 devices in a mesh: slab: 4 (over z), half: 2 (over core), img: 4 (over y, x).
Axes of the slice: x: 2, y: 2, z: 4, core: 2. Of those that a mesh axis runs over, the one named last changes fastest.
Arguments:
- samples: bfloat16 [2048, 2, 96, 128], P(('half', 'slab', 'img')), parts along dimension 0, may hold values from -6 to 6
- kernels: bfloat16 [64, 128, 128], replicated, may hold values from -0.5 to 0.5
- dest: int32 [2048, 1], P(('half', 'slab', 'img')), parts along dimension 0, may hold values from 0 to 3; in each aligned block of 64 rows (0 to 63, 64 to 127, ...) at most 32 rows name the same one
- plane_off: int32 [2048], P(('half', 'slab', 'img')), parts along dimension 0, may hold values from 0 to 127
- kernel_id: int32 [2048], P(('half', 'slab', 'img')), parts along dimension 0, may hold values from 0 to 63
Outputs:
- volume: float32 [2, 192, 512, 512], P(None, ('half', 'img'), 'slab'), parts along dimension 1
There are 2 independent parts, one for each index of `half`. A program takes and returns all parts, laid end to end along the dimension named above; an argument that names none is the same for every part. Nothing has to cross between parts.
Inputs may be any that keep to these rules, and one draw needn't show every extreme that they name: `dest`: in each aligned block of 64 rows (the slice blocks of one device) no slab is named by more than 32 rows.
All inputs are finite; a program needn't handle non-finite values.
Results may differ from a plain program's by a relative error of at most 0.0003.
Values may be sent and summed in bfloat16 or wider, within the bound.
A program may use at most 128 MiB of HBM per device.

v0:
```python
import math

import jax
import jax.numpy as jnp
from jax import lax
from jax.sharding import PartitionSpec as P

NY = 512
NZ = 512


def partner_2(array, axis, bit):
    return lax.ppermute(array, axis, [(i, i ^ 1 << bit) for i in range(lax.axis_size(axis))])


def reverse_bits(values, levels):
    total = values * 0
    for level in range(levels):
        total = total + values // 2**level % 2 * 2 ** (levels - 1 - level)
    return total


def cosine_sine(row_index, col_index, period, factor):
    angle = (
        2.0
        * math.pi
        / period
        * (row_index[:, None] * col_index[None, :] % period).astype(jnp.float32)
    )
    return (factor * jnp.cos(angle), factor * jnp.sin(angle))


def place_cells(tags, z_local, y_blocks):
    plane_hit = tags[:, 0][None, None, :] == jnp.arange(z_local, dtype=jnp.int32)[:, None, None]
    block_hit = tags[:, 1][None, None, :] == jnp.arange(y_blocks, dtype=jnp.int32)[None, :, None]
    return (plane_hit & block_hit & (tags[:, 3][None, None, :] == 1)).astype(jnp.float32)


def per_device(samples, kernels, dest, plane_off, kernel_id):
    exact_mode = lax.Precision.HIGHEST
    n_slab = lax.axis_size("slab")
    n_img = lax.axis_size("img")
    levels = n_slab.bit_length() - 1
    items = samples.shape[0]
    x_rows = samples.shape[2]
    k_width = samples.shape[3]
    y_blocks = NY // k_width
    z_local = NZ // n_slab
    x_share = x_rows // n_img
    capacity = max(2, 2 * items // n_slab)
    slots = n_slab * capacity
    route = dest[:, 0]
    owners = jnp.arange(n_slab, dtype=jnp.int32)
    member = (route[:, None] == owners[None, :]).astype(jnp.int32)
    placing = jnp.sum((jnp.cumsum(member, axis=0) - member) * member, axis=1)
    target = route * capacity + placing
    item_ids = jnp.arange(items, dtype=jnp.int32)
    slot_item = jnp.zeros((slots,), jnp.int32).at[target].set(item_ids)
    slot_live = jnp.zeros((slots,), jnp.int32).at[target].set(1)
    block_id = item_ids % y_blocks
    labels = jnp.stack(
        [plane_off[slot_item], block_id[slot_item], kernel_id[slot_item], slot_live], axis=1
    ).reshape(n_slab, capacity, 4)
    live_mask = slot_live.astype(jnp.bfloat16)[:, None, None, None]
    packed = (samples[slot_item] * live_mask).reshape(n_slab, capacity, 2, x_rows, k_width)
    row_pieces = packed.reshape(n_slab, capacity, 2, n_img, x_share, k_width)
    row_pieces = row_pieces.transpose(0, 3, 1, 2, 4, 5).reshape(
        n_slab * n_img, capacity, 2, x_share, k_width
    )
    label_copies = jnp.broadcast_to(labels[:, None], (n_slab, n_img, capacity, 4)).reshape(
        n_slab * n_img, capacity, 4
    )
    all_slots = n_slab * n_img * capacity
    arrived, tags = (
        lax.all_to_all(row_pieces, ("slab", "img"), split_axis=0, concat_axis=0, tiled=True),
        lax.all_to_all(label_copies, ("slab", "img"), split_axis=0, concat_axis=0, tiled=True),
    )
    arrived = arrived.reshape(all_slots, 2, x_share, k_width)
    tags = tags.reshape(all_slots, 4)
    tables = kernels[tags[:, 2]]
    spread_rows = jnp.einsum("mrxk,mkj->mrxj", arrived, tables, preferred_element_type=jnp.float32)
    cells = place_cells(tags, z_local, y_blocks)
    placed = jnp.einsum("lbm,mrxj->xlrbj", cells, spread_rows, precision=exact_mode)
    grid = placed.reshape(x_share, z_local, 2, NY)
    y_index = jnp.arange(NY, dtype=jnp.int32)
    y_cos, y_sin = cosine_sine(y_index, y_index, NY, 1.0 / math.sqrt(NY * NZ))
    real_part = grid[:, :, 0, :]
    imag_part = grid[:, :, 1, :]
    y_real = jnp.einsum("xly,yv->xlv", real_part, y_cos, precision=exact_mode) - jnp.einsum(
        "xly,yv->xlv", imag_part, y_sin, precision=exact_mode
    )
    y_imag = jnp.einsum("xly,yv->xlv", real_part, y_sin, precision=exact_mode) + jnp.einsum(
        "xly,yv->xlv", imag_part, y_cos, precision=exact_mode
    )
    slab_index = lax.axis_index("slab")
    l_index = jnp.arange(z_local, dtype=jnp.int32)
    z_cos, z_sin = cosine_sine(l_index, l_index, z_local, 1.0)
    local_real = jnp.einsum("xlv,lj->xjv", y_real, z_cos, precision=exact_mode) - jnp.einsum(
        "xlv,lj->xjv", y_imag, z_sin, precision=exact_mode
    )
    local_imag = jnp.einsum("xlv,lj->xjv", y_real, z_sin, precision=exact_mode) + jnp.einsum(
        "xlv,lj->xjv", y_imag, z_cos, precision=exact_mode
    )
    flipped = reverse_bits(slab_index, levels)
    angle = 2.0 * math.pi / NZ * (flipped * l_index).astype(jnp.float32)
    twist_cos = jnp.cos(angle)[None, :, None]
    twist_sin = jnp.sin(angle)[None, :, None]
    state = jnp.stack(
        [
            local_real * twist_cos - local_imag * twist_sin,
            local_real * twist_sin + local_imag * twist_cos,
        ]
    )
    for level in range(levels):
        half_size = 2**level
        upper = slab_index // half_size % 2
        phase = math.pi / half_size * (slab_index % half_size).astype(jnp.float32)
        partner = partner_2(state, "slab", level)
        lower_value = jnp.where(upper == 0, state, partner)
        upper_value = jnp.where(upper == 0, partner, state)
        rotated = jnp.stack(
            [
                jnp.cos(phase) * upper_value[0] - jnp.sin(phase) * upper_value[1],
                jnp.sin(phase) * upper_value[0] + jnp.cos(phase) * upper_value[1],
            ]
        )
        state = jnp.where(upper == 0, lower_value + rotated, lower_value - rotated)
    return state


def solution(mesh):
    in_specs = (
        P(("half", "slab", "img"), None, None, None),
        P(),
        P(("half", "slab", "img"), None),
        P(("half", "slab", "img")),
        P(("half", "slab", "img")),
    )
    out_specs = P(None, ("half", "img"), "slab", None)
    return jax.shard_map(
        per_device, mesh=mesh, in_specs=in_specs, out_specs=out_specs, check_vma=False
    )
```

profile of v0, /device:TPU:0, one launch (start us, length us, event | category | flops | bytes accessed | tf_op | source)
XLA Modules:
  0.0 1245.7 jit_solution(16607415557946169183)
XLA Ops:
  5.4 1.6 gather_fusion.3
  7.0 1.6 gather_fusion.1
  9.5 8.3 all-to-all-start.1
  18.0 4.1 gather_fusion
  22.0 3.3 multiply_bitcast_fusion
  25.3 4.2 copy.20
  29.5 7.1 all-to-all-start
  38.1 13.9 %gather_fusion.4 = bf16[512,128,128]{2,1,0:T(8,128)(2,1)} fusion(bf16[64,128,128]{2,1,0:T(8,128)(2,1)S(1)} %copy-done.4, s32[1024]{0:T(1024)S(1)} %pad_clamp_fusion), kind=kCustom, calls=%fused_computation.4 | custom fusion | bytes 33556480 | tf_op jit(solution)/shard_map/gather | solution.py:80
  52.1 101.3 %all-to-all-done = bf16[16,32,2,24,128]{4,3,2,1,0:T(8,128)(2,1)} async-done(((bf16[16,32,2,24,128]{4,3,2,1,0:T(8,128)(2,1)}), bf16[16,32,2,24,128]{4,3,2,1,0:T(8,128)(2,1)}, u32[]{:S(2)}, u32[]{:S(2)}) %all-to-all-start) | async-done | bytes 6291488 | tf_op jit(solution)/shard_map/all_to_all | solution.py:75
  153.4 10.0 fusion.8
  163.4 22.5 %fusion.2 = f32[2,24,128,128,4]{3,2,4,1,0:T(8,128)S(1)} fusion(f32[512,2,24,128,1]{3,2,1,0,4:T(8,128)S(1)} %fusion.8, pred[512]{0:T(512)(128)(4,1)S(1)} %compare_reduce_fusion, pred[4,512]{1,0:T(4,128)(4,1)S(1)} %iota_compare_fusion.2, pred[128,512]{1,0:T(8,128)(4,1)S(1)} %iota_compare_fusion), kind=kOutput, calls=%fused_computation.12 | convolution fusion | flops 19327877120 | bytes 25233920 | tf_op jit(solution)/shard_map/lbm,mrxj->xlrbj/dot_general | solution.py:83
  185.9 27.6 %fusion.6 = f32[24,128,512]{2,1,0:T(8,128)} fusion(f32[24,128,2,512]{1,3,0,2:T(8,128)S(1)} %bitcast.84), kind=kOutput, calls=%fused_computation.29 | convolution fusion | flops 9667608576 | bytes 12582912 | tf_op jit(solution)/shard_map/xly,yv->xlv/dot_general | solution.py:92
  213.5 27.0 %fusion.4 = f32[24,128,512]{2,1,0:T(8,128)} fusion(f32[24,128,2,512]{1,3,0,2:T(8,128)S(1)} %bitcast.85), kind=kOutput, calls=%fused_computation.27 | convolution fusion | flops 9667608576 | bytes 12582912 | tf_op jit(solution)/shard_map/xly,yv->xlv/dot_general | solution.py:92
  240.5 14.9 %fusion.5 = f32[24,128,512]{2,1,0:T(8,128)S(1)} fusion(f32[24,128,2,512]{1,3,0,2:T(8,128)S(1)} %bitcast.86), kind=kOutput, calls=%fused_computation.28 | convolution fusion | flops 9667608576 | bytes 12582912 | tf_op jit(solution)/shard_map/xly,yv->xlv/dot_general | solution.py:89
  255.5 14.4 %fusion.7 = f32[24,128,512]{2,1,0:T(8,128)S(1)} fusion(f32[24,128,2,512]{1,3,0,2:T(8,128)S(1)} %bitcast.87), kind=kOutput, calls=%fused_computation.30 | convolution fusion | flops 9667608576 | bytes 12582912 | tf_op jit(solution)/shard_map/xly,yv->xlv/dot_general | solution.py:89
  269.9 12.9 %fusion.11 = f32[128,24,512]{2,0,1:T(8,128)} fusion(f32[24,128,512]{2,1,0:T(8,128)} %fusion.4, f32[24,128,512]{2,1,0:T(8,128)} %fusion.6), kind=kOutput, calls=%fused_computation.32 | convolution fusion | flops 2417721344 | bytes 18874368 | tf_op jit(solution)/shard_map/xlv,lj->xjv/dot_general | solution.py:101
  282.9 10.7 fusion.13
  293.6 8.1 fusion.15
  301.7 15.4 %subtract_bitcast_fusion = (f32[1,24,128,512]{3,2,1,0:T(8,128)}, f32[1,24,128,512]{3,2,1,0:T(8,128)}) fusion(f32[128]{0:T(128)S(1)} %get-tuple-element.14, f32[128]{0:T(128)S(1)} %get-tuple-element.15, f32[128,24,512]{2,0,1:T(8,128)} %fusion.15, f32[128,24,512]{2,0,1:T(8,128)} %fusion.11, f32[128,24,512]{2,0,1:T(8,128)} %fusion.13, ...), kind=kOutput, calls=%fused_computation.23 | convolution fusion | flops 2430304256 | bytes 44041216 | tf_op jit(solution)/shard_map/xlv,lj->xjv/dot_general | solution.py:98
  317.1 12.0 pad_maximum_fusion
  329.2 20.3 %collective-permute-start = (f32[2,24,128,512]{3,2,1,0:T(8,128)}, f32[2,24,128,512]{3,2,1,0:T(8,128)}, u32[]{:S(2)}, u32[]{:S(2)}) collective-permute-start(f32[2,24,128,512]{3,2,1,0:T(8,128)} %pad_maximum_fusion), channel_id=1, source_target_pairs={{0,8},{8,0},{16,24},{24,16},{1,9},{9,1},{17,25},{25,17},{2,10},{10... | collective-permute-start | bytes 37748744 | tf_op jit(solution)/shard_map/ppermute | solution.py:13
  349.4 268.9 %collective-permute-done = f32[2,24,128,512]{3,2,1,0:T(8,128)} collective-permute-done((f32[2,24,128,512]{3,2,1,0:T(8,128)}, f32[2,24,128,512]{3,2,1,0:T(8,128)}, u32[]{:S(2)}, u32[]{:S(2)}) %collective-permute-start) | collective-permute-done | bytes 12582944 | tf_op jit(solution)/shard_map/ppermute | solution.py:13
  618.3 14.6 %broadcast_select_fusion = f32[2,24,128,512]{3,2,1,0:T(8,128)} fusion(f32[2,24,128,512]{3,2,1,0:T(8,128)} %collective-permute-done, pred[]{:T(512)S(6)} %eq.93, f32[1,24,128,512]{3,2,1,0:T(8,128)} %get-tuple-element.6, f32[1,24,128,512]{3,2,1,0:T(8,128)} %get-tuple-element.5), kind=kLoop, calls=%fused_computation.25 | loop fusion | flops 6291456 | bytes 37748736 | tf_op jit(solution)/shard_map/jit(_where)/select_n | solution.py:120
  632.9 7.4 multiply_subtract_fusion.1
  640.3 2.2 copy-done.2
  642.5 3.2 copy-done.3
  645.7 10.1 subtract_select_fusion.1
  655.9 3.6 collective-permute-start.1
  659.7 537.4 %collective-permute-done.1 = f32[2,24,128,512]{3,2,1,0:T(8,128)} collective-permute-done((f32[2,24,128,512]{3,2,1,0:T(8,128)}, f32[2,24,128,512]{3,2,1,0:T(8,128)}, u32[]{:S(2)}, u32[]{:S(2)}) %collective-permute-start.1) | collective-permute-done | bytes 12582944 | tf_op jit(solution)/shard_map/ppermute | solution.py:13
  1197.1 19.3 %broadcast_select_fusion.1 = f32[2,24,128,512]{3,2,1,0:T(8,128)} fusion(f32[2,24,128,512]{3,2,1,0:T(8,128)} %collective-permute-done.1, pred[]{:T(512)S(6)} %eq.92, f32[1,24,128,512]{3,2,1,0:T(8,128)} %get-tuple-element.10, f32[1,24,128,512]{3,2,1,0:T(8,128)} %copy-done.5, f32[2,24,128,512]{3,2,1,0:T(8,128)} %collective-permute-done, ...), kind=kLoop, calls=%fused_computation.26 | loop fusion | flops 22020096 | bytes 62914560 | tf_op jit(solution)/shard_map/jit(_where)/select_n | solution.py:120
  1216.5 8.4 multiply_subtract_fusion
  1224.9 20.5 %subtract_select_fusion = f32[2,24,128,512]{3,2,1,0:T(8,128)} fusion(f32[1,24,128,512]{3,2,1,0:T(8,128)} %get-tuple-element.8, f32[1,24,128,512]{3,2,1,0:T(8,128)} %get-tuple-element.7, f32[2,24,128,512]{3,2,1,0:T(8,128)} %collective-permute-done.1, pred[]{:T(512)S(6)} %eq.92, f32[1,24,128,512]{3,2,1,0:T(8,128)} %get-tuple-element.10, ...), kind=kLoop, calls=%fused_computation.14 | loop fusion | flops 34603008 | bytes 75497472 | tf_op jit(solution)/shard_map/jit(_where)/select_n | solution.py:127
  (46 shorter events, 8.0 us)
Async XLA Ops:
  0.0 18.0 %copy-start = (bf16[64,2,96,128]{3,2,1,0:T(8,128)(2,1)S(1)}, bf16[64,2,96,128]{3,2,1,0:T(8,128)(2,1)}, u32[]{:S(2)}) copy-start(bf16[64,2,96,128]{3,2,1,0:T(8,128)(2,1)} %param.5) | copy-start | bytes 9437188
  9.5 19.9 %all-to-all-start.1 = ((s32[16,1,128]{2,1,0:T(1,128)}), s32[16,1,128]{2,1,0:T(1,128)S(1)}, u32[]{:S(2)}, u32[]{:S(2)}) async-start(s32[16,1,128]{2,1,0:T(1,128)} %reshape.176), calls=%async_computation.1 | async-start | bytes 16384 | tf_op jit(solution)/shard_map/all_to_all | solution.py:76
  29.5 8.6 copy-start.4
  29.5 123.9 %all-to-all-start = ((bf16[16,32,2,24,128]{4,3,2,1,0:T(8,128)(2,1)}), bf16[16,32,2,24,128]{4,3,2,1,0:T(8,128)(2,1)}, u32[]{:S(2)}, u32[]{:S(2)}) async-start(bf16[16,32,2,24,128]{4,3,2,1,0:T(8,128)(2,1)} %bitcast.88), calls=%async_computation | async-start | bytes 12582912 | tf_op jit(solution)/shard_map/all_to_all | solution.py:75
  269.9 23.7 %copy-start.6 = (f32[24,128,512]{2,1,0:T(8,128)}, f32[24,128,512]{2,1,0:T(8,128)S(1)}, u32[]{:S(2)}) copy-start(f32[24,128,512]{2,1,0:T(8,128)S(1)} %fusion.7) | copy-start | bytes 18874372
  329.2 289.2 %collective-permute-start = (f32[2,24,128,512]{3,2,1,0:T(8,128)}, f32[2,24,128,512]{3,2,1,0:T(8,128)}, u32[]{:S(2)}, u32[]{:S(2)}) collective-permute-start(f32[2,24,128,512]{3,2,1,0:T(8,128)} %pad_maximum_fusion), channel_id=1, source_target_pairs={{0,8},{8,0},{16,24},{24,16},{1,9},{9,1},{17,25},{25,17},{2,10},{10... | collective-permute-start | bytes 37748744 | tf_op jit(solution)/shard_map/ppermute | solution.py:13
  632.9 9.6 copy-start.2
  632.9 12.8 %copy-start.3 = (f32[1,24,128,512]{3,2,1,0:T(8,128)S(1)}, f32[1,24,128,512]{3,2,1,0:T(8,128)}, u32[]{:S(2)}) copy-start(f32[1,24,128,512]{3,2,1,0:T(8,128)} %get-tuple-element.6) | copy-start | bytes 18874372
  640.3 15.6 %copy-start.5 = (f32[1,24,128,512]{3,2,1,0:T(8,128)}, f32[1,24,128,512]{3,2,1,0:T(8,128)S(1)}, u32[]{:S(2)}) copy-start(f32[1,24,128,512]{3,2,1,0:T(8,128)S(1)} %get-tuple-element.9) | copy-start | bytes 18874372
  655.9 541.3 %collective-permute-start.1 = (f32[2,24,128,512]{3,2,1,0:T(8,128)}, f32[2,24,128,512]{3,2,1,0:T(8,128)}, u32[]{:S(2)}, u32[]{:S(2)}) collective-permute-start(f32[2,24,128,512]{3,2,1,0:T(8,128)} %subtract_select_fusion.1), channel_id=1, source_target_pairs={{0,16},{8,24},{16,0},{24,8},{1,17},{9,25},{17,1},{25,9},{2,18},{10... | collective-permute-start | bytes 37748744 | tf_op jit(solution)/shard_map/ppermute | solution.py:13
  1224.9 20.5 %copy-start.1 = (bf16[64,2,96,128]{3,2,1,0:T(8,128)(2,1)S(1)}, bf16[64,2,96,128]{3,2,1,0:T(8,128)(2,1)}, u32[]{:S(2)}) copy-start(bf16[64,2,96,128]{3,2,1,0:T(8,128)(2,1)} %param.5) | copy-start | bytes 9437188
where the time goes:
time: 1260 us; the launch traced here: 1250 us
  waiting for transfers between devices  908 us (72%)
  matrix products  164 us (13%)
  other arithmetic  99 us (8%)
  starting transfers between devices  39.3 us (3%)
  local copies, waits for them, and re-layouts  35.4 us (3%)
    ppermute x2, waiting for transfers between devices, partner_2(): lax.ppermute(array, axis, [(i, i ^ 1 << bit) for i in range(lax.axis_size...  806 us
    all_to_all x1, waiting for transfers between devices, per_device(): lax.all_to_all(row_pieces, ('slab', 'img'), split_axis=0, concat_axis=0,...  101 us
    select_n x2, other arithmetic, per_device(): upper_value = jnp.where(upper == 0, partner, state)  33.9 us
    select_n x2, other arithmetic, per_device(): state = jnp.where(upper == 0, lower_value + rotated, lower_value - rotated)  30.6 us
    dot_general x1, matrix products, per_device(): jnp.einsum('xly,yv->xlv', imag_part, y_cos, precision=exact_mode)  27.6 us
    dot_general x1, matrix products, per_device(): jnp.einsum('xly,yv->xlv', real_part, y_sin, precision=exact_mode)  27 us
  transfers between devices with their start and end apart: 4, of which 3 were waited for; matrix products, arithmetic and copies ran while one was open for 2% of the time, Pallas kernels for 0%

commit v1 on v0

v1 whole, which is shorter than its diff:
```python
import functools
import math

import jax
import jax.numpy as jnp
import numpy as np
from jax import lax
from jax.experimental import pallas as pl
from jax.experimental.pallas import tpu as pltpu
from jax.sharding import PartitionSpec as P

NY = 512
NZ = 512
ROWS = 8
PAIR = 2


def reverse_bits(values, levels):
    total = values * 0
    for level in range(levels):
        total = total + values // 2**level % 2 * 2 ** (levels - 1 - level)
    return total


def y_matrix():
    index = np.arange(NY)
    angle = 2.0 * np.pi / NY * (index[:, None] * index[None, :] % NY)
    c, s = np.cos(angle), np.sin(angle)
    full = np.block([[c, s], [-s, c]]) / math.sqrt(NY * NZ)
    full = full.astype(np.float32)
    high = full.astype(jnp.bfloat16)
    low = (full - high.astype(np.float32)).astype(jnp.bfloat16)
    return high, low


def split(value):
    high = value.astype(jnp.bfloat16)
    low = (value - high.astype(jnp.float32)).astype(jnp.bfloat16)
    return high, low


def chunk_kernel(first, last, y_blocks, z_local, *refs):
    kid_ref, block_ref, table_ref, weight_ref = refs[:4]
    refs = refs[4:]
    if not first:
        before_ref, refs = refs[0], refs[1:]
    if last:
        y_high_ref, y_low_ref = refs[:2]
        out_ref, spread_ref, total_ref = refs[-3:]
    else:
        total_ref, spread_ref = refs
    items, rows, width = block_ref.shape
    per_block = items // y_blocks
    group = 4

    @pl.when(pl.program_id(0) == 0)
    def _():
        def body(step, carry):
            for u in range(group):
                for b in range(y_blocks):
                    q = step * group + u
                    item = q * y_blocks + b
                    value = jnp.dot(
                        block_ref[item],
                        table_ref[kid_ref[item]],
                        preferred_element_type=jnp.float32,
                    )
                    place = pl.multiple_of((b * per_block + q) * rows, rows)
                    spread_ref[pl.ds(place, rows), :] = value
            return carry

        lax.fori_loop(0, per_block // group, body, 0)

    x_first = pl.program_id(0) * PAIR
    for b in range(y_blocks):
        parts = []
        for x in range(PAIR):
            base = b * per_block * rows + x_first + x
            real = spread_ref[pl.ds(base, per_block, stride=rows), :]
            imag = spread_ref[pl.ds(base + rows // 2, per_block, stride=rows), :]
            parts.append(jnp.concatenate([real, imag], axis=0))
        high, low = split(jnp.concatenate(parts, axis=1))
        value = jnp.dot(
            weight_ref[b],
            jnp.concatenate([high, low, high], axis=0),
            preferred_element_type=jnp.float32,
        )
        for x in range(PAIR):
            for part in range(2):
                piece = value[
                    part * z_local : (part + 1) * z_local, x * width : (x + 1) * width
                ]
                at = (
                    slice(x * z_local, (x + 1) * z_local),
                    slice(part * NY + b * width, part * NY + (b + 1) * width),
                )
                if not first:
                    piece = piece + before_ref[at]
                total_ref[at] = piece
    if last:
        high, low = split(total_ref[...])
        for part in range(2):
            columns = slice(part * NY, (part + 1) * NY)
            result = (
                jnp.dot(high, y_high_ref[:, columns], preferred_element_type=jnp.float32)
                + jnp.dot(low, y_high_ref[:, columns], preferred_element_type=jnp.float32)
                + jnp.dot(high, y_low_ref[:, columns], preferred_element_type=jnp.float32)
            )
            for x in range(PAIR):
                out_ref[part, x] = result[x * z_local : (x + 1) * z_local]


def run_chunk(kid, block, table, weight, before, out, y_parts, chunk, last, sizes):
    y_blocks, z_local, x_share = sizes
    items, rows, width = block.shape
    steps = ROWS // PAIR
    first = before is None

    def whole(array):
        zeros = (0,) * array.ndim
        return pl.BlockSpec(array.shape, lambda i: zeros, pipeline_mode=pl.Buffered(1))

    total_spec = pl.BlockSpec((PAIR * z_local, 2 * NY), lambda i: (i, 0))
    args = [kid, block, table, weight]
    specs = [pl.BlockSpec(memory_space=pltpu.SMEM)] + [whole(a) for a in args[1:]]
    if not first:
        args.append(before)
        specs.append(total_spec)
    aliases = {}
    spread = pltpu.VMEM((items * rows, width), jnp.float32)
    if last:
        args += y_parts
        specs += [whole(a) for a in y_parts]
        if out is not None:
            aliases = {len(args): 0}
            args.append(out)
            specs.append(pl.BlockSpec(memory_space=pl.ANY))
        out_shape = jax.ShapeDtypeStruct((2, x_share, z_local, NY), jnp.float32)
        out_spec = pl.BlockSpec(
            (2, PAIR, z_local, NY), lambda i: (0, chunk * steps + i, 0, 0)
        )
        scratch = [spread, pltpu.VMEM((PAIR * z_local, 2 * NY), jnp.float32)]
    else:
        out_shape = jax.ShapeDtypeStruct((ROWS * z_local, 2 * NY), jnp.float32)
        out_spec = total_spec
        scratch = [spread]
    flops = 2 * items * rows * width * width + 2 * 3 * 2 * z_local * 2 * items * ROWS * width
    if last:
        flops += 2 * 3 * ROWS * z_local * 4 * NY * NY
    return pl.pallas_call(
        functools.partial(chunk_kernel, first, last, y_blocks, z_local),
        grid=(steps,),
        in_specs=specs,
        out_specs=out_spec,
        out_shape=out_shape,
        scratch_shapes=scratch,
        input_output_aliases=aliases,
        compiler_params=pltpu.CompilerParams(vmem_limit_bytes=40 * 2**20),
        cost_estimate=pl.CostEstimate(
            flops=flops, bytes_accessed=16 * 2**20, transcendentals=0
        ),
    )(*args)


def per_device(samples, kernels, dest, plane_off, kernel_id):
    n_slab = lax.axis_size("slab")
    n_img = lax.axis_size("img")
    levels = n_slab.bit_length() - 1
    items, _, x_rows, k_width = samples.shape
    y_blocks = NY // k_width
    z_local = NZ // n_slab
    x_share = x_rows // n_img
    chunks = x_share // ROWS
    sizes = (y_blocks, z_local, x_share)
    slab, img = lax.axis_index("slab"), lax.axis_index("img")

    planes = n_slab * plane_off + reverse_bits(dest[:, 0], levels)
    meta = lax.all_gather(jnp.stack([planes, kernel_id], axis=0), ("slab", "img"))
    meta = meta.reshape(n_slab, n_img, 2, items)
    meta = meta[(slab - jnp.arange(n_slab)) % n_slab][:, img ^ jnp.arange(n_img)]
    meta = meta.transpose(0, 2, 1, 3).reshape(n_slab, 2, n_img * items)
    kid = meta[:, 1]
    z_of = meta[:, 0].reshape(n_slab, n_img * items // y_blocks, y_blocks).transpose(0, 2, 1)
    z_out = slab * z_local + jnp.arange(z_local, dtype=jnp.int32)
    turn = z_out[None, None, :, None] * z_of[:, :, None, :] % NZ
    angle = 2.0 * math.pi / NZ * turn.astype(jnp.float32)
    c, s = jnp.cos(angle), jnp.sin(angle)
    weight = jnp.concatenate(
        [jnp.concatenate([c, -s], axis=3), jnp.concatenate([s, c], axis=3)], axis=2
    )
    high = lax.reduce_precision(weight, 8, 7)
    low = (weight - high).astype(jnp.bfloat16)
    high = high.astype(jnp.bfloat16)
    weight = jnp.concatenate([high, high, low], axis=3)
    y_parts = [jnp.asarray(a) for a in y_matrix()]

    def rows_for(owner, chunk):
        piece = lax.dynamic_slice_in_dim(samples, owner * x_share + chunk * ROWS, ROWS, axis=2)
        return piece.reshape(items, 2 * ROWS, k_width)

    ring = [(i, (i + 1) % n_slab) for i in range(n_slab)]
    blocks = []
    for chunk in range(chunks):
        pieces = [rows_for(img, chunk)]
        for k in range(1, n_img):
            pairs = [(i, i ^ k) for i in range(n_img)]
            pieces.append(lax.ppermute(rows_for(img ^ k, chunk), "img", pairs))
        held = [jnp.concatenate(pieces, axis=0)]
        for _ in range(1, n_slab):
            held.append(lax.ppermute(held[-1], "slab", ring))
        blocks.append(held)

    out = None
    for chunk in range(chunks):
        total = None
        for step in range(n_slab):
            last = step == n_slab - 1
            value = run_chunk(
                kid[step], blocks[chunk][step], kernels, weight[step], total, out,
                y_parts, chunk, last, sizes,
            )
            if last:
                out = value
            else:
                total = value
    return out


def solution(mesh):
    in_specs = (
        P(("half", "slab", "img"), None, None, None),
        P(),
        P(("half", "slab", "img"), None),
        P(("half", "slab", "img")),
        P(("half", "slab", "img")),
    )
    out_specs = P(None, ("half", "img"), "slab", None)
    return jax.shard_map(
        per_device, mesh=mesh, in_specs=in_specs, out_specs=out_specs, check_vma=False
    )
```

time: 1260 us -> 279 us (0.22); the launches traced: 1250 us -> 279 us
  waiting for transfers between devices: 908 us -> 27 us
  matrix products: 164 us -> 0 us
  Pallas kernels: 0 us -> 113 us
  blocking collectives: 0 us -> 93.5 us
  other arithmetic: 99 us -> 7.63 us
  local copies, waits for them, and re-layouts: 35.4 us -> 14.3 us
  starting transfers between devices: 39.3 us -> 22.6 us
    ppermute x2 -> x18, waiting for transfers between devices: 806 us -> 27 us  [the longest x9 27 us: per_device(): pieces.append(lax.ppermute(rows_for(img ^ k, chunk), 'img', pairs))]
    dot_general x10 -> x0, matrix products: 164 us -> none  [the longest x1 27.6 us: per_device(): jnp.einsum('xly,yv->xlv', imag_part, y_cos, precision=exact_mode)]
    pallas_call x0 -> x12, Pallas kernels: none -> 113 us  [run_chunk(): pl.pallas_call(functools.partial(chunk_kernel, first, last, y_blocks, z_l...]
    all_to_all x2 -> x0, waiting for transfers between devices: 101 us -> none  [the longest x1 101 us: per_device(): lax.all_to_all(row_pieces, ('slab', 'img'), split_axis=0, concat_axis=0,...]
    all_gather x0 -> x1, blocking collectives: none -> 93.5 us  [per_device(): lax.all_gather(jnp.stack([planes, kernel_id], axis=0), ('slab', 'img'))]
    select_n x7 -> x2, other arithmetic: 65.3 us -> 0.02 us  [per_device(): meta[(slab - jnp.arange(n_slab)) % n_slab][:, img ^ jnp.arange(n_img)]]
    gather x5 -> x3, local copies, waits for them, and re-layouts: 22.4 us -> 1.15 us  [per_device(): meta[(slab - jnp.arange(n_slab)) % n_slab][:, img ^ jnp.arange(n_img)]]
    sub x2 -> x0, other arithmetic: 15.8 us -> none  [per_device(): jnp.cos(phase) * upper_value[0] - jnp.sin(phase) * upper_value[1]]
  transfers between devices with their start and end apart: 4 -> 18, of which waited for: 3 -> 6; matrix products, arithmetic and copies ran while one was open for 2% -> 4% of each run, Pallas kernels for 0% -> 35%
where the time goes in v1:
time: 279 us
  Pallas kernels  113 us (41%)
  blocking collectives  93.5 us (34%)
  waiting for transfers between devices  27 us (10%)
  starting transfers between devices  22.6 us (8%)
  local copies, waits for them, and re-layouts  14.3 us (5%)
  other arithmetic  7.63 us (3%)
    pallas_call x12, Pallas kernels, run_chunk(): pl.pallas_call(functools.partial(chunk_kernel, first, last, y_blocks, z_l...  113 us
    all_gather x1, blocking collectives, per_device(): lax.all_gather(jnp.stack([planes, kernel_id], axis=0), ('slab', 'img'))  93.5 us
    ppermute x9, waiting for transfers between devices, per_device(): pieces.append(lax.ppermute(rows_for(img ^ k, chunk), 'img', pairs))  27 us
    ppermute x9, starting transfers between devices, per_device(): held.append(lax.ppermute(held[-1], 'slab', ring))  11.5 us
    ppermute x9, starting transfers between devices, per_device(): pieces.append(lax.ppermute(rows_for(img ^ k, chunk), 'img', pairs))  11.1 us
    unnamed x38, local copies, waits for them, and re-layouts  8.22 us
  transfers between devices with their start and end apart: 18, of which 6 were waited for; matrix products, arithmetic and copies ran while one was open for 4% of the time, Pallas kernels for 35%

profile of v1, /device:TPU:0, one launch (start us, length us, event | category | flops | bytes accessed | tf_op | source)
XLA Modules:
  0.0 278.9 jit_solution(14471944300385626748)
XLA Ops:
  0.0 3.2 %dynamic-slice_bitcast_fusion.3 = (bf16[64,16,128]{2,1,0:T(8,128)(2,1)S(1)}, bf16[64,16,128]{2,1,0:T(8,128)(2,1)S(1)}, bf16[64,16,128]{2,1,0:T(8,128)(2,1)S(1)},...) fusion(bf16[64,2,96,128]{3,2,1,0:T(8,128)(2,1)} %param.7, ...), kind=kLoop, calls=%fused_computation.28 | loop fusion | bytes 6291504 | tf_op jit(solution)/shard_map/reshape | solution.py:199
  3.3 2.9 %collective-permute-start.12 = (bf16[64,16,128]{2,1,0:T(8,128)(2,1)S(1)}, bf16[64,16,128]{2,1,0:T(8,128)(2,1)S(1)}, u32[]{:S(2)}, u32[]{:S(2)}) collective-permute-start(bf16[64,16,128]{2,1,0:T(8,128)(2,1)S(1)} %get-tuple-element.6), channel_id=1, source_target_pairs={{0,1},{1,0},{2,3},{3,2},{4,5},{5,4},{6,7},{7,6},{8,9},{9,8},{10,11... | collective-permute-start | bytes 786440 | tf_op jit(solution)/shard_map/ppermute | solution.py:207
  6.2 1.5 collective-permute-start.13
  7.7 5.6 %collective-permute-done.12 = bf16[64,16,128]{2,1,0:T(8,128)(2,1)S(1)} collective-permute-done((bf16[64,16,128]{2,1,0:T(8,128)(2,1)S(1)}, bf16[64,16,128]{2,1,0:T(8,128)(2,1)S(1)}, u32[]{:S(2)}, u32[]{:S(2)}) %collective-permute-start.12) | collective-permute-done | bytes 262176 | tf_op jit(solution)/shard_map/ppermute | solution.py:207
  13.3 6.3 %collective-permute-done.13 = bf16[64,16,128]{2,1,0:T(8,128)(2,1)S(1)} collective-permute-done((bf16[64,16,128]{2,1,0:T(8,128)(2,1)S(1)}, bf16[64,16,128]{2,1,0:T(8,128)(2,1)S(1)}, u32[]{:S(2)}, u32[]{:S(2)}) %collective-permute-start.13) | collective-permute-done | bytes 262176 | tf_op jit(solution)/shard_map/ppermute | solution.py:207
  19.7 1.6 collective-permute-start.15
  26.1 4.5 %collective-permute-done.6 = bf16[64,16,128]{2,1,0:T(8,128)(2,1)S(1)} collective-permute-done((bf16[64,16,128]{2,1,0:T(8,128)(2,1)S(1)}, bf16[64,16,128]{2,1,0:T(8,128)(2,1)S(1)}, u32[]{:S(2)}, u32[]{:S(2)}) %collective-permute-start.6) | collective-permute-done | bytes 262176 | tf_op jit(solution)/shard_map/ppermute | solution.py:207
  30.6 1.5 collective-permute-start.1
  32.1 5.5 %collective-permute-done.7 = bf16[64,16,128]{2,1,0:T(8,128)(2,1)} collective-permute-done((bf16[64,16,128]{2,1,0:T(8,128)(2,1)S(1)}, bf16[64,16,128]{2,1,0:T(8,128)(2,1)}, u32[]{:S(2)}, u32[]{:S(2)}) %collective-permute-start.7) | collective-permute-done | bytes 262176 | tf_op jit(solution)/shard_map/ppermute | solution.py:207
  39.2 1.6 collective-permute-start.9
  41.9 4.1 %collective-permute-done.1 = bf16[64,16,128]{2,1,0:T(8,128)(2,1)S(1)} collective-permute-done((bf16[64,16,128]{2,1,0:T(8,128)(2,1)S(1)}, bf16[64,16,128]{2,1,0:T(8,128)(2,1)S(1)}, u32[]{:S(2)}, u32[]{:S(2)}) %collective-permute-start.1) | collective-permute-done | bytes 262176 | tf_op jit(solution)/shard_map/ppermute | solution.py:207
  47.1 1.6 collective-permute-start.3
  48.8 1.6 collective-permute-start.16
  50.4 93.5 %all-gather.1 = s32[16,2,64]{2,1,0:T(2,128)S(1)} all-gather(s32[1,2,64]{2,1,0:T(2,128)S(1)} %add_bitcast_fusion), channel_id=2, replica_groups=mesh['slab'=4,'half'=2,'img'=4] {'slab','img'}, dimensions={0}, use_global_device_ids=true | all-gather | bytes 8704 | tf_op jit(solution)/shard_map/all_gather | solution.py:178
  145.4 4.2 %fusion.6 = (f32[4,4,128,64]{3,2,1,0:T(8,128)S(1)}, f32[4,4,128,64]{3,2,1,0:T(8,128)S(1)}, f32[4,4,128,64]{3,2,1,0:T(8,128)S(1)}) fusion(s32[4,4,64]{2,1,0:T(4,128)S(1)} %copy.25, s32[128]{0:T(128)S(1)} %iota_add_fusion), kind=kLoop, calls=%fused_computation.24 | loop fusion | flops 1966080 | bytes 1577472 | tf_op jit(solution)/shard_map/neg | solution.py:189
  152.5 6.9 %shard_map.79.refs_4_ = f32[1024,1024]{1,0:T(8,128)S(1)} custom-call(s32[256]{0:T(256)S(1)} %bitcast.69, bf16[256,16,128]{2,1,0:T(8,128)(2,1)S(1)} %pad_maximum_fusion.3.refs_1_, bf16[64,128,128]{2,1,0:T(8,128)(2,1)S(1)} %copy-done, bf16[4,256,384]{2,1,0:T(8,128)(2,1)S(1)} %get-tuple-element.17.refs_3_), custom_call_target="tpu_custom_call" | custom-call | flops 939524096 | bytes 16777216 | tf_op jit(solution)/shard_map/pallas_call | solution.py:150
  159.5 6.9 %shard_map.76.refs_4_ = f32[1024,1024]{1,0:T(8,128)S(1)} custom-call(s32[256]{0:T(256)S(1)} %bitcast.70, bf16[256,16,128]{2,1,0:T(8,128)(2,1)S(1)} %copy-done.13, bf16[64,128,128]{2,1,0:T(8,128)(2,1)S(1)} %copy-done, bf16[4,256,384]{2,1,0:T(8,128)(2,1)S(1)} %get-tuple-element.17.refs_3_), custom_call_target="tpu_custom_call" | custom-call | flops 939524096 | bytes 16777216 | tf_op jit(solution)/shard_map/pallas_call | solution.py:150
  166.4 6.9 %shard_map.73.refs_4_ = f32[1024,1024]{1,0:T(8,128)S(1)} custom-call(s32[256]{0:T(256)S(1)} %bitcast.71, bf16[256,16,128]{2,1,0:T(8,128)(2,1)S(1)} %copy-done.15, bf16[64,128,128]{2,1,0:T(8,128)(2,1)S(1)} %copy-done, bf16[4,256,384]{2,1,0:T(8,128)(2,1)S(1)} %get-tuple-element.17.refs_3_), custom_call_target="tpu_custom_call" | custom-call | flops 939524096 | bytes 16777216 | tf_op jit(solution)/shard_map/pallas_call | solution.py:150
  173.3 2.0 copy-done.3
  175.3 7.6 %shard_map.80.refs_4_ = f32[1024,1024]{1,0:T(8,128)S(1)} custom-call(s32[256]{0:T(256)S(1)} %bitcast.66, bf16[256,16,128]{2,1,0:T(8,128)(2,1)} %collective-permute-done.15.refs_1_, bf16[64,128,128]{2,1,0:T(8,128)(2,1)S(1)} %copy-done, bf16[4,256,384]{2,1,0:T(8,128)(2,1)S(1)} %get-tuple-element.18.refs_3_, f32[1024,1024]{1,0:T(8,128)S(1)} %shard_map.79.refs_4_), custom_call_target="tpu_custom_call" | custom-call | flops 939524096 | bytes 16777216 | tf_op jit(solution)/shard_map/pallas_call | solution.py:150
  183.0 4.8 %collective-permute-start.11 = (bf16[256,16,128]{2,1,0:T(8,128)(2,1)}, bf16[256,16,128]{2,1,0:T(8,128)(2,1)}, u32[]{:S(2)}, u32[]{:S(2)}) collective-permute-start(bf16[256,16,128]{2,1,0:T(8,128)(2,1)} %collective-permute-done.10.refs_1_), channel_id=1, source_target_pairs={{0,8},{8,16},{16,24},{24,0},{1,9},{9,17},{17,25},{25,1},{2,10},{10... | collective-permute-start | bytes 3145736 | tf_op jit(solution)/shard_map/ppermute | solution.py:210
  187.7 7.6 %shard_map.77.refs_4_ = f32[1024,1024]{1,0:T(8,128)S(1)} custom-call(s32[256]{0:T(256)S(1)} %bitcast.67, bf16[256,16,128]{2,1,0:T(8,128)(2,1)} %collective-permute-done.9.refs_1_, bf16[64,128,128]{2,1,0:T(8,128)(2,1)S(1)} %copy-done, bf16[4,256,384]{2,1,0:T(8,128)(2,1)S(1)} %get-tuple-element.18.refs_3_, f32[1024,1024]{1,0:T(8,128)S(1)} %shard_map.76.refs_4_), custom_call_target="tpu_custom_call" | custom-call | flops 939524096 | bytes 16777216 | tf_op jit(solution)/shard_map/pallas_call | solution.py:150
  195.4 2.2 copy-done.4
  197.5 8.4 %shard_map.74.refs_4_ = f32[1024,1024]{1,0:T(8,128)S(1)} custom-call(s32[256]{0:T(256)S(1)} %bitcast.68, bf16[256,16,128]{2,1,0:T(8,128)(2,1)} %collective-permute-done.3.refs_1_, bf16[64,128,128]{2,1,0:T(8,128)(2,1)S(1)} %copy-done, bf16[4,256,384]{2,1,0:T(8,128)(2,1)S(1)} %get-tuple-element.18.refs_3_, f32[1024,1024]{1,0:T(8,128)S(1)} %copy-done.4), custom_call_target="tpu_custom_call" | custom-call | flops 939524096 | bytes 16777216 | tf_op jit(solution)/shard_map/pallas_call | solution.py:150
  206.1 7.8 %shard_map.81.refs_4_ = f32[1024,1024]{1,0:T(8,128)S(1)} custom-call(s32[256]{0:T(256)S(1)} %bitcast.63, bf16[256,16,128]{2,1,0:T(8,128)(2,1)} %collective-permute-done.16.refs_1_, bf16[64,128,128]{2,1,0:T(8,128)(2,1)S(1)} %copy-done, bf16[4,256,384]{2,1,0:T(8,128)(2,1)S(1)} %get-tuple-element.19.refs_3_, f32[1024,1024]{1,0:T(8,128)S(1)} %shard_map.80.refs_4_), custom_call_target="tpu_custom_call" | custom-call | flops 939524096 | bytes 16777216 | tf_op jit(solution)/shard_map/pallas_call | solution.py:150
  213.8 2.0 copy-done.10
  215.9 7.6 %shard_map.78.refs_4_ = f32[1024,1024]{1,0:T(8,128)S(1)} custom-call(s32[256]{0:T(256)S(1)} %bitcast.64, bf16[256,16,128]{2,1,0:T(8,128)(2,1)} %collective-permute-done.10.refs_1_, bf16[64,128,128]{2,1,0:T(8,128)(2,1)S(1)} %copy-done, bf16[4,256,384]{2,1,0:T(8,128)(2,1)S(1)} %get-tuple-element.19.refs_3_, f32[1024,1024]{1,0:T(8,128)S(1)} %copy-done.2), custom_call_target="tpu_custom_call" | custom-call | flops 939524096 | bytes 16777216 | tf_op jit(solution)/shard_map/pallas_call | solution.py:150
  223.5 8.6 %shard_map.75.refs_4_ = f32[1024,1024]{1,0:T(8,128)S(1)} custom-call(s32[256]{0:T(256)S(1)} %bitcast.65, bf16[256,16,128]{2,1,0:T(8,128)(2,1)} %collective-permute-done.4.refs_1_, bf16[64,128,128]{2,1,0:T(8,128)(2,1)S(1)} %copy-done, bf16[4,256,384]{2,1,0:T(8,128)(2,1)S(1)} %get-tuple-element.19.refs_3_, f32[1024,1024]{1,0:T(8,128)S(1)} %shard_map.74.refs_4_), custom_call_target="tpu_custom_call" | custom-call | flops 939524096 | bytes 16777216 | tf_op jit(solution)/shard_map/pallas_call | solution.py:150
  232.2 1.6 copy-done.8
  233.8 15.3 %shard_map.82.refs_7_ = f32[2,24,128,512]{3,2,1,0:T(8,128)} custom-call(s32[256]{0:T(256)S(1)} %bitcast.72, bf16[256,16,128]{2,1,0:T(8,128)(2,1)} %collective-permute-done.17.refs_1_, bf16[64,128,128]{2,1,0:T(8,128)(2,1)S(1)} %copy-done, bf16[4,256,384]{2,1,0:T(8,128)(2,1)S(1)} %copy-done.9, f32[1024,1024]{1,0:T(8,128)S(1)} %copy-done.11, ...), custom_call_target="tpu_custom_call" | custom-call | flops 7381975040 | bytes 16777216 | tf_op jit(solution)/shard_map/pallas_call | solution.py:150
  249.2 15.2 %shard_map.83.refs_7_ = f32[2,24,128,512]{3,2,1,0:T(8,128)} custom-call(s32[256]{0:T(256)S(1)} %bitcast.73, bf16[256,16,128]{2,1,0:T(8,128)(2,1)} %collective-permute-done.11.refs_1_, bf16[64,128,128]{2,1,0:T(8,128)(2,1)S(1)} %copy-done, bf16[4,256,384]{2,1,0:T(8,128)(2,1)S(1)} %copy-done.9, ...), custom_call_target="tpu_custom_call", output_to_operand_aliasing={{}: (7, {})} | custom-call | flops 7381975040 | bytes 16777216 | tf_op jit(solution)/shard_map/pallas_call | solution.py:150
  264.4 14.5 %shard_map.84 = f32[2,24,128,512]{3,2,1,0:T(8,128)} custom-call(s32[256]{0:T(256)S(1)} %bitcast.74, bf16[256,16,128]{2,1,0:T(8,128)(2,1)S(1)} %collective-permute-done.5.refs_1_, bf16[64,128,128]{2,1,0:T(8,128)(2,1)S(1)} %copy-done, bf16[4,256,384]{2,1,0:T(8,128)(2,1)S(1)} %copy-done.9, ...), custom_call_target="tpu_custom_call", output_to_operand_aliasing={{}: (7, {})} | custom-call | flops 7381975040 | bytes 16777216 | tf_op jit(solution)/shard_map/pallas_call | solution.py:150
  (80 shorter events, 13.2 us)
Async XLA Ops:
  0.0 26.1 %copy-start.17 = (s32[64,1]{0,1:T(1,128)S(1)}, s32[64,1]{0,1:T(1,128)}, u32[]{:S(2)}) copy-start(s32[64,1]{0,1:T(1,128)} %param.9) | copy-start | bytes 772
  0.0 26.1 %copy-start.18 = (s32[64]{0:T(128)S(1)}, s32[64]{0:T(128)}, u32[]{:S(2)}) copy-start(s32[64]{0:T(128)} %param.10) | copy-start | bytes 772
  0.0 26.1 %copy-start.16 = (s32[64]{0:T(128)S(1)}, s32[64]{0:T(128)}, u32[]{:S(2)}) copy-start(s32[64]{0:T(128)} %param.11) | copy-start | bytes 772
  3.3 10.1 %collective-permute-start.12 = (bf16[64,16,128]{2,1,0:T(8,128)(2,1)S(1)}, bf16[64,16,128]{2,1,0:T(8,128)(2,1)S(1)}, u32[]{:S(2)}, u32[]{:S(2)}) collective-permute-start(bf16[64,16,128]{2,1,0:T(8,128)(2,1)S(1)} %get-tuple-element.6), channel_id=1, source_target_pairs={{0,1},{1,0},{2,3},{3,2},{4,5},{5,4},{6,7},{7,6},{8,9},{9,8},{10,11... | collective-permute-start | bytes 786440 | tf_op jit(solution)/shard_map/ppermute | solution.py:207
  6.2 13.4 %collective-permute-start.13 = (bf16[64,16,128]{2,1,0:T(8,128)(2,1)S(1)}, bf16[64,16,128]{2,1,0:T(8,128)(2,1)S(1)}, u32[]{:S(2)}, u32[]{:S(2)}) collective-permute-start(bf16[64,16,128]{2,1,0:T(8,128)(2,1)S(1)} %get-tuple-element.16), channel_id=1, source_target_pairs={{0,2},{1,3},{2,0},{3,1},{4,6},{5,7},{6,4},{7,5},{8,10},{9,11},{10,... | collective-permute-start | bytes 786440 | tf_op jit(solution)/shard_map/ppermute | solution.py:207
  7.7 11.9 %collective-permute-start.14 = (bf16[64,16,128]{2,1,0:T(8,128)(2,1)S(1)}, bf16[64,16,128]{2,1,0:T(8,128)(2,1)S(1)}, u32[]{:S(2)}, u32[]{:S(2)}) collective-permute-start(bf16[64,16,128]{2,1,0:T(8,128)(2,1)S(1)} %get-tuple-element.15), channel_id=1, source_target_pairs={{0,3},{1,2},{2,1},{3,0},{4,7},{5,6},{6,5},{7,4},{8,11},{9,10},{10,... | collective-permute-start | bytes 786440 | tf_op jit(solution)/shard_map/ppermute | solution.py:207
  19.7 29.1 %collective-permute-start.15 = (bf16[256,16,128]{2,1,0:T(8,128)(2,1)S(1)}, bf16[256,16,128]{2,1,0:T(8,128)(2,1)}, u32[]{:S(2)}, u32[]{:S(2)}) collective-permute-start(bf16[256,16,128]{2,1,0:T(8,128)(2,1)S(1)} %pad_maximum_fusion.3.refs_1_), channel_id=1, source_target_pairs={{0,8},{8,16},{16,24},{24,0},{1,9},{9,17},{17,25},{25,1},{2,10},{10... | collective-permute-start | bytes 3145736 | tf_op jit(solution)/shard_map/ppermute | solution.py:210
  21.3 9.2 %collective-permute-start.6 = (bf16[64,16,128]{2,1,0:T(8,128)(2,1)S(1)}, bf16[64,16,128]{2,1,0:T(8,128)(2,1)S(1)}, u32[]{:S(2)}, u32[]{:S(2)}) collective-permute-start(bf16[64,16,128]{2,1,0:T(8,128)(2,1)S(1)} %get-tuple-element.9), channel_id=1, source_target_pairs={{0,1},{1,0},{2,3},{3,2},{4,5},{5,4},{6,7},{7,6},{8,9},{9,8},{10,11... | collective-permute-start | bytes 786440 | tf_op jit(solution)/shard_map/ppermute | solution.py:207
  22.6 15.0 %collective-permute-start.7 = (bf16[64,16,128]{2,1,0:T(8,128)(2,1)S(1)}, bf16[64,16,128]{2,1,0:T(8,128)(2,1)}, u32[]{:S(2)}, u32[]{:S(2)}) collective-permute-start(bf16[64,16,128]{2,1,0:T(8,128)(2,1)S(1)} %get-tuple-element.8), channel_id=1, source_target_pairs={{0,2},{1,3},{2,0},{3,1},{4,6},{5,7},{6,4},{7,5},{8,10},{9,11},{10,... | collective-permute-start | bytes 786440 | tf_op jit(solution)/shard_map/ppermute | solution.py:207
  23.4 14.6 %collective-permute-start.8 = (bf16[64,16,128]{2,1,0:T(8,128)(2,1)S(1)}, bf16[64,16,128]{2,1,0:T(8,128)(2,1)}, u32[]{:S(2)}, u32[]{:S(2)}) collective-permute-start(bf16[64,16,128]{2,1,0:T(8,128)(2,1)S(1)} %get-tuple-element.7), channel_id=1, source_target_pairs={{0,3},{1,2},{2,1},{3,0},{4,7},{5,6},{6,5},{7,4},{8,11},{9,10},{10,... | collective-permute-start | bytes 786440 | tf_op jit(solution)/shard_map/ppermute | solution.py:207
  24.8 17.1 %collective-permute-start = (bf16[64,16,128]{2,1,0:T(8,128)(2,1)}, bf16[64,16,128]{2,1,0:T(8,128)(2,1)}, u32[]{:S(2)}, u32[]{:S(2)}) collective-permute-start(bf16[64,16,128]{2,1,0:T(8,128)(2,1)} %get-tuple-element.13), channel_id=1, source_target_pairs={{0,1},{1,0},{2,3},{3,2},{4,5},{5,4},{6,7},{7,6},{8,9},{9,8},{10,11... | collective-permute-start | bytes 786440 | tf_op jit(solution)/shard_map/ppermute | solution.py:207
  30.6 15.5 %collective-permute-start.1 = (bf16[64,16,128]{2,1,0:T(8,128)(2,1)S(1)}, bf16[64,16,128]{2,1,0:T(8,128)(2,1)S(1)}, u32[]{:S(2)}, u32[]{:S(2)}) collective-permute-start(bf16[64,16,128]{2,1,0:T(8,128)(2,1)S(1)} %get-tuple-element.12), channel_id=1, source_target_pairs={{0,2},{1,3},{2,0},{3,1},{4,6},{5,7},{6,4},{7,5},{8,10},{9,11},{10,... | collective-permute-start | bytes 786440 | tf_op jit(solution)/shard_map/ppermute | solution.py:207
  37.6 8.5 %collective-permute-start.2 = (bf16[64,16,128]{2,1,0:T(8,128)(2,1)S(1)}, bf16[64,16,128]{2,1,0:T(8,128)(2,1)S(1)}, u32[]{:S(2)}, u32[]{:S(2)}) collective-permute-start(bf16[64,16,128]{2,1,0:T(8,128)(2,1)S(1)} %get-tuple-element.11), channel_id=1, source_target_pairs={{0,3},{1,2},{2,1},{3,0},{4,7},{5,6},{6,5},{7,4},{8,11},{9,10},{10,... | collective-permute-start | bytes 786440 | tf_op jit(solution)/shard_map/ppermute | solution.py:207
  39.2 111.1 %copy-start.12 = (bf16[256,16,128]{2,1,0:T(8,128)(2,1)}, bf16[256,16,128]{2,1,0:T(8,128)(2,1)S(1)}, u32[]{:S(2)}) copy-start(bf16[256,16,128]{2,1,0:T(8,128)(2,1)S(1)} %pad_maximum_fusion.2.refs_1_) | copy-start | bytes 3145732
  39.2 111.1 %collective-permute-start.9 = (bf16[256,16,128]{2,1,0:T(8,128)(2,1)S(1)}, bf16[256,16,128]{2,1,0:T(8,128)(2,1)}, u32[]{:S(2)}, u32[]{:S(2)}) collective-permute-start(bf16[256,16,128]{2,1,0:T(8,128)(2,1)S(1)} %pad_maximum_fusion.2.refs_1_), channel_id=1, source_target_pairs={{0,8},{8,16},{16,24},{24,0},{1,9},{9,17},{17,25},{25,1},{2,10},{10... | collective-permute-start | bytes 3145736 | tf_op jit(solution)/shard_map/ppermute | solution.py:210
  47.1 103.1 %copy-start.14 = (bf16[256,16,128]{2,1,0:T(8,128)(2,1)}, bf16[256,16,128]{2,1,0:T(8,128)(2,1)S(1)}, u32[]{:S(2)}) copy-start(bf16[256,16,128]{2,1,0:T(8,128)(2,1)S(1)} %pad_maximum_fusion.1.refs_1_) | copy-start | bytes 3145732
  47.1 103.6 %collective-permute-start.3 = (bf16[256,16,128]{2,1,0:T(8,128)(2,1)S(1)}, bf16[256,16,128]{2,1,0:T(8,128)(2,1)}, u32[]{:S(2)}, u32[]{:S(2)}) collective-permute-start(bf16[256,16,128]{2,1,0:T(8,128)(2,1)S(1)} %pad_maximum_fusion.1.refs_1_), channel_id=1, source_target_pairs={{0,8},{8,16},{16,24},{24,0},{1,9},{9,17},{17,25},{25,1},{2,10},{10... | collective-permute-start | bytes 3145736 | tf_op jit(solution)/shard_map/ppermute | solution.py:210
  48.8 102.0 %collective-permute-start.16 = (bf16[256,16,128]{2,1,0:T(8,128)(2,1)}, bf16[256,16,128]{2,1,0:T(8,128)(2,1)}, u32[]{:S(2)}, u32[]{:S(2)}) collective-permute-start(bf16[256,16,128]{2,1,0:T(8,128)(2,1)} %collective-permute-done.15.refs_1_), channel_id=1, source_target_pairs={{0,8},{8,16},{16,24},{24,0},{1,9},{9,17},{17,25},{25,1},{2,10},{10... | collective-permute-start | bytes 3145736 | tf_op jit(solution)/shard_map/ppermute | solution.py:210
  150.3 32.7 %collective-permute-start.10 = (bf16[256,16,128]{2,1,0:T(8,128)(2,1)}, bf16[256,16,128]{2,1,0:T(8,128)(2,1)}, u32[]{:S(2)}, u32[]{:S(2)}) collective-permute-start(bf16[256,16,128]{2,1,0:T(8,128)(2,1)} %collective-permute-done.9.refs_1_), channel_id=1, source_target_pairs={{0,8},{8,16},{16,24},{24,0},{1,9},{9,17},{17,25},{25,1},{2,10},{10... | collective-permute-start | bytes 3145736 | tf_op jit(solution)/shard_map/ppermute | solution.py:210
  150.7 55.2 %collective-permute-start.4 = (bf16[256,16,128]{2,1,0:T(8,128)(2,1)}, bf16[256,16,128]{2,1,0:T(8,128)(2,1)}, u32[]{:S(2)}, u32[]{:S(2)}) collective-permute-start(bf16[256,16,128]{2,1,0:T(8,128)(2,1)} %collective-permute-done.3.refs_1_), channel_id=1, source_target_pairs={{0,8},{8,16},{16,24},{24,0},{1,9},{9,17},{17,25},{25,1},{2,10},{10... | collective-permute-start | bytes 3145736 | tf_op jit(solution)/shard_map/ppermute | solution.py:210
  150.8 81.4 %collective-permute-start.17 = (bf16[256,16,128]{2,1,0:T(8,128)(2,1)}, bf16[256,16,128]{2,1,0:T(8,128)(2,1)}, u32[]{:S(2)}, u32[]{:S(2)}) collective-permute-start(bf16[256,16,128]{2,1,0:T(8,128)(2,1)} %collective-permute-done.16.refs_1_), channel_id=1, source_target_pairs={{0,8},{8,16},{16,24},{24,0},{1,9},{9,17},{17,25},{25,1},{2,10},{10... | collective-permute-start | bytes 3145736 | tf_op jit(solution)/shard_map/ppermute | solution.py:210
  152.5 6.9 %copy-start.13 = (bf16[256,16,128]{2,1,0:T(8,128)(2,1)S(1)}, bf16[256,16,128]{2,1,0:T(8,128)(2,1)}, u32[]{:S(2)}) copy-start(bf16[256,16,128]{2,1,0:T(8,128)(2,1)} %copy-done.12) | copy-start | bytes 3145732
  159.4 6.9 %copy-start.15 = (bf16[256,16,128]{2,1,0:T(8,128)(2,1)S(1)}, bf16[256,16,128]{2,1,0:T(8,128)(2,1)}, u32[]{:S(2)}) copy-start(bf16[256,16,128]{2,1,0:T(8,128)(2,1)} %copy-done.14) | copy-start | bytes 3145732
  183.0 66.2 %collective-permute-start.11 = (bf16[256,16,128]{2,1,0:T(8,128)(2,1)}, bf16[256,16,128]{2,1,0:T(8,128)(2,1)}, u32[]{:S(2)}, u32[]{:S(2)}) collective-permute-start(bf16[256,16,128]{2,1,0:T(8,128)(2,1)} %collective-permute-done.10.refs_1_), channel_id=1, source_target_pairs={{0,8},{8,16},{16,24},{24,0},{1,9},{9,17},{17,25},{25,1},{2,10},{10... | collective-permute-start | bytes 3145736 | tf_op jit(solution)/shard_map/ppermute | solution.py:210
  197.5 8.4 %copy-start.1 = (f32[1024,1024]{1,0:T(8,128)}, f32[1024,1024]{1,0:T(8,128)S(1)}, u32[]{:S(2)}) copy-start(f32[1024,1024]{1,0:T(8,128)S(1)} %shard_map.77.refs_4_) | copy-start | bytes 12582916
  205.9 58.4 %collective-permute-start.5 = (bf16[256,16,128]{2,1,0:T(8,128)(2,1)}, bf16[256,16,128]{2,1,0:T(8,128)(2,1)S(1)}, u32[]{:S(2)}, u32[]{:S(2)}) collective-permute-start(bf16[256,16,128]{2,1,0:T(8,128)(2,1)} %collective-permute-done.4.refs_1_), channel_id=1, source_target_pairs={{0,8},{8,16},{16,24},{24,0},{1,9},{9,17},{17,25},{25,1},{2,10},{10... | collective-permute-start | bytes 3145736 | tf_op jit(solution)/shard_map/ppermute | solution.py:210
  206.1 9.8 %copy-start.2 = (f32[1024,1024]{1,0:T(8,128)S(1)}, f32[1024,1024]{1,0:T(8,128)}, u32[]{:S(2)}) copy-start(f32[1024,1024]{1,0:T(8,128)} %copy-done.1) | copy-start | bytes 12582916
  223.5 8.7 %copy-start.5 = (f32[1024,1024]{1,0:T(8,128)}, f32[1024,1024]{1,0:T(8,128)S(1)}, u32[]{:S(2)}) copy-start(f32[1024,1024]{1,0:T(8,128)S(1)} %shard_map.78.refs_4_) | copy-start | bytes 12582916
  223.5 8.7 %copy-start.7 = (bf16[1024,1024]{1,0:T(8,128)(2,1)S(1)}, bf16[1024,1024]{1,0:T(8,128)(2,1)}, u32[]{:S(2)}) copy-start(bf16[1024,1024]{1,0:T(8,128)(2,1)} %constant.107.clone.refs_5_) | copy-start | bytes 6291460
  223.5 8.7 %copy-start.9 = (bf16[4,256,384]{2,1,0:T(8,128)(2,1)S(1)}, bf16[4,256,384]{2,1,0:T(8,128)(2,1)}, u32[]{:S(2)}) copy-start(bf16[4,256,384]{2,1,0:T(8,128)(2,1)} %get-tuple-element.20.refs_3_) | copy-start | bytes 2359300
  223.5 8.7 %copy-start.11 = (f32[1024,1024]{1,0:T(8,128)S(1)}, f32[1024,1024]{1,0:T(8,128)}, u32[]{:S(2)}) copy-start(f32[1024,1024]{1,0:T(8,128)} %copy-done.10) | copy-start | bytes 12582916
  233.8 15.3 %copy-start.6 = (f32[1024,1024]{1,0:T(8,128)S(1)}, f32[1024,1024]{1,0:T(8,128)}, u32[]{:S(2)}) copy-start(f32[1024,1024]{1,0:T(8,128)} %copy-done.5) | copy-start | bytes 12582916
  (5 other events, 9.6 us)

commit v2 on v1

--- a/solution.py
+++ b/solution.py
@@ -40,8 +40,8 @@
 
 
 def chunk_kernel(first, last, y_blocks, z_local, *refs):
-    kid_ref, block_ref, table_ref, weight_ref = refs[:4]
-    refs = refs[4:]
+    kid_ref, own_ref, other_ref, table_ref, weight_ref = refs[:5]
+    refs = refs[5:]
     if not first:
         before_ref, refs = refs[0], refs[1:]
     if last:
@@ -49,12 +49,12 @@
         out_ref, spread_ref, total_ref = refs[-3:]
     else:
         total_ref, spread_ref = refs
-    items, rows, width = block_ref.shape
-    per_block = items // y_blocks
+    own, rows, width = own_ref.shape
+    others = other_ref.shape[0]
+    per_block = (own + others) // y_blocks
     group = 4
 
-    @pl.when(pl.program_id(0) == 0)
-    def _():
+    def spread_items(block_ref, first_item):
         def body(step, carry):
             for u in range(group):
                 for b in range(y_blocks):
@@ -62,14 +62,19 @@
                     item = q * y_blocks + b
                     value = jnp.dot(
                         block_ref[item],
-                        table_ref[kid_ref[item]],
+                        table_ref[kid_ref[first_item + item]],
                         preferred_element_type=jnp.float32,
                     )
-                    place = pl.multiple_of((b * per_block + q) * rows, rows)
-                    spread_ref[pl.ds(place, rows), :] = value
+                    place = b * per_block + first_item // y_blocks + q
+                    spread_ref[pl.ds(pl.multiple_of(place * rows, rows), rows), :] = value
             return carry
 
-        lax.fori_loop(0, per_block // group, body, 0)
+        lax.fori_loop(0, block_ref.shape[0] // (y_blocks * group), body, 0)
+
+    @pl.when(pl.program_id(0) == 0)
+    def _():
+        spread_items(own_ref, 0)
+        spread_items(other_ref, own)
 
     x_first = pl.program_id(0) * PAIR
     for b in range(y_blocks):
@@ -110,9 +115,10 @@
                 out_ref[part, x] = result[x * z_local : (x + 1) * z_local]
 
 
-def run_chunk(kid, block, table, weight, before, out, y_parts, chunk, last, sizes):
+def run_chunk(kid, own, other, table, weight, before, out, y_parts, chunk, last, sizes):
     y_blocks, z_local, x_share = sizes
-    items, rows, width = block.shape
+    rows, width = other.shape[1:]
+    items = own.shape[1] + other.shape[0]
     steps = ROWS // PAIR
     first = before is None
 
@@ -121,8 +127,11 @@
         return pl.BlockSpec(array.shape, lambda i: zeros, pipeline_mode=pl.Buffered(1))
 
     total_spec = pl.BlockSpec((PAIR * z_local, 2 * NY), lambda i: (i, 0))
-    args = [kid, block, table, weight]
-    specs = [pl.BlockSpec(memory_space=pltpu.SMEM)] + [whole(a) for a in args[1:]]
+    args = [kid, own, other, table, weight]
+    own_spec = pl.BlockSpec(
+        (None, *own.shape[1:]), lambda i: (chunk, 0, 0, 0), pipeline_mode=pl.Buffered(1)
+    )
+    specs = [pl.BlockSpec(memory_space=pltpu.SMEM), own_spec] + [whole(a) for a in args[2:]]
     if not first:
         args.append(before)
         specs.append(total_spec)
@@ -175,10 +184,19 @@
     slab, img = lax.axis_index("slab"), lax.axis_index("img")
 
     planes = n_slab * plane_off + reverse_bits(dest[:, 0], levels)
-    meta = lax.all_gather(jnp.stack([planes, kernel_id], axis=0), ("slab", "img"))
-    meta = meta.reshape(n_slab, n_img, 2, items)
-    meta = meta[(slab - jnp.arange(n_slab)) % n_slab][:, img ^ jnp.arange(n_img)]
-    meta = meta.transpose(0, 2, 1, 3).reshape(n_slab, 2, n_img * items)
+    labels = jnp.stack([planes, kernel_id], axis=0)
+    ring = [(i, (i + 1) % n_slab) for i in range(n_slab)]
+
+    def shift(array, step):
+        return lax.ppermute(array, "slab", [(i, (i + step) % n_slab) for i in range(n_slab)])
+
+    def swap(array, k):
+        return lax.ppermute(array, "img", [(i, i ^ k) for i in range(n_img)])
+
+    by_step = jnp.stack([labels] + [shift(labels, t) for t in range(1, n_slab)])
+    by_step, samples = lax.optimization_barrier((by_step, samples))
+    meta = jnp.stack([by_step] + [swap(by_step, k) for k in range(1, n_img)])
+    meta = meta.transpose(1, 2, 0, 3).reshape(n_slab, 2, n_img * items)
     kid = meta[:, 1]
     z_of = meta[:, 0].reshape(n_slab, n_img * items // y_blocks, y_blocks).transpose(0, 2, 1)
     z_out = slab * z_local + jnp.arange(z_local, dtype=jnp.int32)
@@ -194,35 +212,65 @@
     weight = jnp.concatenate([high, high, low], axis=3)
     y_parts = [jnp.asarray(a) for a in y_matrix()]
 
-    def rows_for(owner, chunk):
-        piece = lax.dynamic_slice_in_dim(samples, owner * x_share + chunk * ROWS, ROWS, axis=2)
-        return piece.reshape(items, 2 * ROWS, k_width)
-
-    ring = [(i, (i + 1) % n_slab) for i in range(n_slab)]
-    blocks = []
+    by_rows = samples.reshape(items, 2, n_img, chunks, ROWS, k_width).transpose(2, 3, 0, 1, 4, 5)
+    by_rows = by_rows.reshape(n_img, chunks, items, 2 * ROWS, k_width)
+
+    def rows_for(owner):
+        return lax.dynamic_index_in_dim(by_rows, owner, 0, keepdims=False)
+
+    own = [rows_for(img)]
+    sends = [rows_for(img ^ k) for k in range(1, n_img)]
+    others = []
     for chunk in range(chunks):
-        pieces = [rows_for(img, chunk)]
-        for k in range(1, n_img):
-            pairs = [(i, i ^ k) for i in range(n_img)]
-            pieces.append(lax.ppermute(rows_for(img ^ k, chunk), "img", pairs))
-        held = [jnp.concatenate(pieces, axis=0)]
-        for _ in range(1, n_slab):
-            held.append(lax.ppermute(held[-1], "slab", ring))
-        blocks.append(held)
-
-    out = None
-    for chunk in range(chunks):
-        total = None
-        for step in range(n_slab):
-            last = step == n_slab - 1
-            value = run_chunk(
-                kid[step], blocks[chunk][step], kernels, weight[step], total, out,
-                y_parts, chunk, last, sizes,
-            )
-            if last:
+        if chunk > 0:
+            sends, others[-1] = lax.optimization_barrier((sends, others[-1]))
+        got = [swap(array[chunk], k + 1) for k, array in enumerate(sends)]
+        others.append([jnp.concatenate(got, axis=0)])
+
+    streams = [own] + others
+    order = sorted(
+        (4 * step + max(0, 7 * n - 5), n, step + 1)
+        for n in range(chunks + 1)
+        for step in range(n_slab - 1)
+    )
+    place = {(n, step): at for at, (_, n, step) in enumerate(order)}
+    total, taken, out = [None] * chunks, [0] * chunks, None
+
+    def work(chunk, out):
+        step = taken[chunk]
+        value = run_chunk(
+            kid[step], own[step], others[chunk][step], kernels, weight[step], total[chunk], out,
+            y_parts, chunk, step == n_slab - 1, sizes,
+        )
+        taken[chunk] = step + 1
+        return value
+
+    for at, (_, n, step) in enumerate(order):
+        send = streams[n][step - 1]
+        if at >= 2:
+            _, m, ahead = order[at - 2]
+            send, streams[m][ahead] = lax.optimization_barrier((send, streams[m][ahead]))
+        for chunk in range(chunks if at >= 3 else 0):
+            step_of = taken[chunk]
+            if step_of == n_slab or any(
+                place.get((k, step_of), 0) > at - 3 for k in (0, chunk + 1)
+            ):
+                continue
+            value = work(chunk, out)
+            send, value = lax.optimization_barrier((send, value))
+            if taken[chunk] == n_slab:
                 out = value
             else:
-                total = value
+                total[chunk] = value
+            break
+        streams[n].append(lax.ppermute(send, "slab", ring))
+    for chunk in range(chunks):
+        while taken[chunk] < n_slab:
+            value = work(chunk, out)
+            if taken[chunk] == n_slab:
+                out = value
+            else:
+                total[chunk] = value
     return out
 
 

time: 279 us -> 248 us (0.89)
  blocking collectives: 93.5 us -> 0 us
  waiting for transfers between devices: 27 us -> 77.8 us
  local copies, waits for them, and re-layouts: 14.3 us -> 22.6 us
  starting transfers between devices: 22.6 us -> 29.3 us
  Pallas kernels: 113 us -> 109 us
    all_gather x1 -> x0, blocking collectives: 93.5 us -> none  [per_device(): lax.all_gather(jnp.stack([planes, kernel_id], axis=0), ('slab', 'img'))]
    ppermute x18 -> x27, waiting for transfers between devices: 27 us -> 77.8 us  [the longest x12 68.2 us: per_device(): streams[n].append(lax.ppermute(send, 'slab', ring))]
    ppermute x18 -> x27, starting transfers between devices: 22.6 us -> 29.3 us  [the longest x12 22.9 us: swap(): return lax.ppermute(array, 'img', [(i, i ^ k) for i in range(n_img)])]
    squeeze x1 -> x9, local copies, waits for them, and re-layouts: 1.28 us -> 6.08 us  [the longest x7 3.13 us: per_device(): got = [swap(array[chunk], k + 1) for k, array in enumerate(sends)]]
    unnamed x38 -> x52, local copies, waits for them, and re-layouts: 8.22 us -> 12.8 us
    pallas_call x12, Pallas kernels: 113 us -> 109 us  [run_chunk(): pl.pallas_call(functools.partial(chunk_kernel, first, last, y_blocks, z_l...]
  transfers between devices with their start and end apart: 18 -> 27, of which waited for: 6 -> 15; matrix products, arithmetic and copies ran while one was open for 4% -> 7% of each run, Pallas kernels for 35% -> 38%
where the time goes in v2:
time: 248 us; the launch traced here: 247 us
  Pallas kernels  109 us (44%)
  waiting for transfers between devices  77.8 us (31%)
  starting transfers between devices  29.3 us (12%)
  local copies, waits for them, and re-layouts  22.6 us (9%)
  other arithmetic  7.85 us (3%)
    pallas_call x12, Pallas kernels, run_chunk(): pl.pallas_call(functools.partial(chunk_kernel, first, last, y_blocks, z_l...  109 us
    ppermute x12, waiting for transfers between devices, per_device(): streams[n].append(lax.ppermute(send, 'slab', ring))  68.2 us
    ppermute x12, starting transfers between devices, swap(): return lax.ppermute(array, 'img', [(i, i ^ k) for i in range(n_img)])  22.9 us
    unnamed x52, local copies, waits for them, and re-layouts  12.8 us
    ppermute x3, starting transfers between devices, shift(): lax.ppermute(array, 'slab', [(i, (i + step) % n_slab) for i in range(n_sl...  6.06 us
    ppermute x12, waiting for transfers between devices, swap(): return lax.ppermute(array, 'img', [(i, i ^ k) for i in range(n_img)])  5.24 us
  transfers between devices with their start and end apart: 27, of which 15 were waited for; matrix products, arithmetic and copies ran while one was open for 7% of the time, Pallas kernels for 38%

profile of v2, /device:TPU:0, one launch (start us, length us, event | category | flops | bytes accessed | tf_op | source)
XLA Modules:
  0.0 247.2 jit_solution(13011927485511173313)
XLA Ops:
  1.4 5.0 %collective-permute-start.2 = (s32[2,64]{1,0:T(2,128)S(1)}, s32[2,64]{1,0:T(2,128)S(1)}, u32[]{:S(2)}, u32[]{:S(2)}) collective-permute-start(s32[2,64]{1,0:T(2,128)S(1)} %get-tuple-element.122), channel_id=1, source_target_pairs={{0,24},{8,0},{16,8},{24,16},{1,25},{9,1},{17,9},{25,17},{2,26},{10... | collective-permute-start | bytes 1544 | tf_op jit(solution)/shard_map/ppermute | solution.py:191
  7.7 3.2 %collective-permute-done.1 = s32[2,64]{1,0:T(2,128)S(1)} collective-permute-done((s32[2,64]{1,0:T(2,128)S(1)}, s32[2,64]{1,0:T(2,128)S(1)}, u32[]{:S(2)}, u32[]{:S(2)}) %collective-permute-start.1) | collective-permute-done | bytes 544 | tf_op jit(solution)/shard_map/ppermute | solution.py:191
  11.8 2.4 collective-permute-start.5
  15.3 2.6 %copy.15 = bf16[64,2,4,3,8,128]{5,4,1,0,3,2:T(8,128)(2,1)S(1)} copy(bf16[64,2,4,3,8,128]{5,4,3,2,1,0:T(8,128)(2,1)} %bitcast.88) | data formatting | bytes 6291456 | tf_op jit(solution)/shard_map/reshape | solution.py:215
  20.5 2.4 collective-permute-start.8
  24.4 4.2 %fusion.6 = (f32[4,4,128,64]{3,2,1,0:T(8,128)S(1)}, f32[4,4,128,64]{3,2,1,0:T(8,128)S(1)}, f32[4,4,128,64]{3,2,1,0:T(8,128)S(1)}) fusion(s32[4,4,64]{2,1,0:T(4,128)S(1)} %copy.13, s32[128]{0:T(128)S(1)} %iota_add_fusion), kind=kLoop, calls=%fused_computation.26 | loop fusion | flops 1966080 | bytes 1577472 | tf_op jit(solution)/shard_map/neg | solution.py:207
  30.9 2.2 collective-permute-done.7
  37.5 6.1 %collective-permute-done.14.refs_1_ = bf16[3,64,16,128]{3,2,1,0:T(8,128)(2,1)S(1)} collective-permute-done((bf16[3,64,16,128]{3,2,1,0:T(8,128)(2,1)S(1)}, bf16[3,64,16,128]{3,2,1,0:T(8,128)(2,1)S(1)}, u32[]{:S(2)}, u32[]{:S(2)}) %collective-permute-start.14) | collective-permute-done | bytes 786464 | tf_op jit(solution)/shard_map/ppermute | solution.py:266
  45.5 3.0 %collective-permute-start.9 = (bf16[64,16,128]{2,1,0:T(8,128)(2,1)S(1)}, bf16[64,16,128]{2,1,0:T(8,128)(2,1)S(1)}, u32[]{:S(2)}, u32[]{:S(2)}) collective-permute-start(bf16[64,16,128]{2,1,0:T(8,128)(2,1)S(1)} %slice_bitcast_fusion.9), channel_id=1, source_target_pairs={{0,1},{1,0},{2,3},{3,2},{4,5},{5,4},{6,7},{7,6},{8,9},{9,8},{10,11... | collective-permute-start | bytes 786440 | tf_op jit(solution)/shard_map/ppermute | solution.py:194
  48.6 6.9 %shard_map.73.refs_5_ = f32[1024,1024]{1,0:T(8,128)S(1)} custom-call(s32[256]{0:T(256)S(1)} %bitcast.80, bf16[3,64,16,128]{3,2,1,0:T(8,128)(2,1)S(1)} %get-tuple-element.107.refs_1_, bf16[192,16,128]{2,1,0:T(8,128)(2,1)S(1)} %pad_maximum_fusion.1.refs_2_, bf16[64,128,128]{2,1,0:T(8,128)(2,1)S(1)} %copy-done, bf16[4,256,384]{2,1,0:T(8,128)(2,1)S(1)} %get-tuple-element.104.refs_4_), custom_call_target="tpu_custom_call" | custom-call | flops 939524096 | bytes 16777216 | tf_op jit(solution)/shard_map/pallas_call | solution.py:159
  55.5 4.9 %collective-permute-done.12.refs_2_ = bf16[192,16,128]{2,1,0:T(8,128)(2,1)S(1)} collective-permute-done((bf16[192,16,128]{2,1,0:T(8,128)(2,1)S(1)}, bf16[192,16,128]{2,1,0:T(8,128)(2,1)S(1)}, u32[]{:S(2)}, u32[]{:S(2)}) %collective-permute-start.12) | collective-permute-done | bytes 786464 | tf_op jit(solution)/shard_map/ppermute | solution.py:266
  60.4 6.9 %shard_map.74.refs_5_ = f32[1024,1024]{1,0:T(8,128)S(1)} custom-call(s32[256]{0:T(256)S(1)} %bitcast.77, bf16[3,64,16,128]{3,2,1,0:T(8,128)(2,1)S(1)} %collective-permute-done.14.refs_1_, bf16[192,16,128]{2,1,0:T(8,128)(2,1)S(1)} %collective-permute-done.12.refs_2_, bf16[64,128,128]{2,1,0:T(8,128)(2,1)S(1)} %copy-done, ...), custom_call_target="tpu_custom_call" | custom-call | flops 939524096 | bytes 16777216 | tf_op jit(solution)/shard_map/pallas_call | solution.py:159
  67.3 9.9 %collective-permute-done.15.refs_1_ = bf16[3,64,16,128]{3,2,1,0:T(8,128)(2,1)S(1)} collective-permute-done((bf16[3,64,16,128]{3,2,1,0:T(8,128)(2,1)S(1)}, bf16[3,64,16,128]{3,2,1,0:T(8,128)(2,1)S(1)}, u32[]{:S(2)}, u32[]{:S(2)}) %collective-permute-start.15) | collective-permute-done | bytes 786464 | tf_op jit(solution)/shard_map/ppermute | solution.py:266
  79.2 3.1 %collective-permute-start.18 = (bf16[64,16,128]{2,1,0:T(8,128)(2,1)S(1)}, bf16[64,16,128]{2,1,0:T(8,128)(2,1)S(1)}, u32[]{:S(2)}, u32[]{:S(2)}) collective-permute-start(bf16[64,16,128]{2,1,0:T(8,128)(2,1)S(1)} %slice_bitcast_fusion.5), channel_id=1, source_target_pairs={{0,2},{1,3},{2,0},{3,1},{4,6},{5,7},{6,4},{7,5},{8,10},{9,11},{10,... | collective-permute-start | bytes 786440 | tf_op jit(solution)/shard_map/ppermute | solution.py:194
  82.4 6.9 %shard_map.76.refs_5_ = f32[1024,1024]{1,0:T(8,128)S(1)} custom-call(s32[256]{0:T(256)S(1)} %bitcast.81, bf16[3,64,16,128]{3,2,1,0:T(8,128)(2,1)S(1)} %copy-done.6, bf16[192,16,128]{2,1,0:T(8,128)(2,1)S(1)} %pad_maximum_fusion.2.refs_2_, bf16[64,128,128]{2,1,0:T(8,128)(2,1)S(1)} %copy-done, bf16[4,256,384]{2,1,0:T(8,128)(2,1)S(1)} %get-tuple-element.104.refs_4_), custom_call_target="tpu_custom_call" | custom-call | flops 939524096 | bytes 16777216 | tf_op jit(solution)/shard_map/pallas_call | solution.py:159
  89.3 4.8 %collective-permute-done.13.refs_2_ = bf16[192,16,128]{2,1,0:T(8,128)(2,1)S(1)} collective-permute-done((bf16[192,16,128]{2,1,0:T(8,128)(2,1)S(1)}, bf16[192,16,128]{2,1,0:T(8,128)(2,1)S(1)}, u32[]{:S(2)}, u32[]{:S(2)}) %collective-permute-start.13) | collective-permute-done | bytes 786464 | tf_op jit(solution)/shard_map/ppermute | solution.py:266
  94.1 6.9 %shard_map.75.refs_5_ = f32[1024,1024]{1,0:T(8,128)S(1)} custom-call(s32[256]{0:T(256)S(1)} %bitcast.74, bf16[3,64,16,128]{3,2,1,0:T(8,128)(2,1)S(1)} %collective-permute-done.15.refs_1_, bf16[192,16,128]{2,1,0:T(8,128)(2,1)S(1)} %collective-permute-done.13.refs_2_, bf16[64,128,128]{2,1,0:T(8,128)(2,1)S(1)} %copy-done, ...), custom_call_target="tpu_custom_call" | custom-call | flops 939524096 | bytes 16777216 | tf_op jit(solution)/shard_map/pallas_call | solution.py:159
  103.0 7.9 %collective-permute-done.16.refs_1_ = bf16[3,64,16,128]{3,2,1,0:T(8,128)(2,1)S(1)} collective-permute-done((bf16[3,64,16,128]{3,2,1,0:T(8,128)(2,1)S(1)}, bf16[3,64,16,128]{3,2,1,0:T(8,128)(2,1)S(1)}, u32[]{:S(2)}, u32[]{:S(2)}) %collective-permute-start.16) | collective-permute-done | bytes 786464 | tf_op jit(solution)/shard_map/ppermute | solution.py:266
  112.1 4.3 %collective-permute-start.19 = (bf16[64,16,128]{2,1,0:T(8,128)(2,1)S(1)}, bf16[64,16,128]{2,1,0:T(8,128)(2,1)S(1)}, u32[]{:S(2)}, u32[]{:S(2)}) collective-permute-start(bf16[64,16,128]{2,1,0:T(8,128)(2,1)S(1)} %slice_bitcast_fusion.4), channel_id=1, source_target_pairs={{0,3},{1,2},{2,1},{3,0},{4,7},{5,6},{6,5},{7,4},{8,11},{9,10},{10,... | collective-permute-start | bytes 786440 | tf_op jit(solution)/shard_map/ppermute | solution.py:194
  117.9 2.9 %collective-permute-done.19 = bf16[64,16,128]{2,1,0:T(8,128)(2,1)S(1)} collective-permute-done((bf16[64,16,128]{2,1,0:T(8,128)(2,1)S(1)}, bf16[64,16,128]{2,1,0:T(8,128)(2,1)S(1)}, u32[]{:S(2)}, u32[]{:S(2)}) %collective-permute-start.19) | collective-permute-done | bytes 262176 | tf_op jit(solution)/shard_map/ppermute | solution.py:194
  121.5 7.6 %shard_map.78.refs_5_ = f32[1024,1024]{1,0:T(8,128)S(1)} custom-call(s32[256]{0:T(256)S(1)} %bitcast.82, bf16[3,64,16,128]{3,2,1,0:T(8,128)(2,1)S(1)} %copy-done.6, bf16[192,16,128]{2,1,0:T(8,128)(2,1)} %constant_dynamic-update-slice_fusion.refs_2_, bf16[64,128,128]{2,1,0:T(8,128)(2,1)S(1)} %copy-done, bf16[4,256,384]{2,1,0:T(8,128)(2,1)S(1)} %get-tuple-element.104.refs_4_), custom_call_target="tpu_custom_call" | custom-call | flops 939524096 | bytes 16777216 | tf_op jit(solution)/shard_map/pallas_call | solution.py:159
  131.1 7.7 %shard_map.77.refs_5_ = f32[1024,1024]{1,0:T(8,128)S(1)} custom-call(s32[256]{0:T(256)S(1)} %bitcast.78, bf16[3,64,16,128]{3,2,1,0:T(8,128)(2,1)S(1)} %copy-done.11, bf16[192,16,128]{2,1,0:T(8,128)(2,1)} %collective-permute-done.21.refs_2_, bf16[64,128,128]{2,1,0:T(8,128)(2,1)S(1)} %copy-done, bf16[4,256,384]{2,1,0:T(8,128)(2,1)S(1)} %get-tuple-element.103.refs_4_, ...), custom_call_target="tpu_custom_call" | custom-call | flops 939524096 | bytes 16777216 | tf_op jit(solution)/shard_map/pallas_call | solution.py:159
  138.8 5.8 %collective-permute-done.20.refs_2_ = bf16[192,16,128]{2,1,0:T(8,128)(2,1)S(1)} collective-permute-done((bf16[192,16,128]{2,1,0:T(8,128)(2,1)S(1)}, bf16[192,16,128]{2,1,0:T(8,128)(2,1)S(1)}, u32[]{:S(2)}, u32[]{:S(2)}) %collective-permute-start.20) | collective-permute-done | bytes 786464 | tf_op jit(solution)/shard_map/ppermute | solution.py:266
  150.0 14.5 %shard_map.80.refs_8_ = f32[2,24,128,512]{3,2,1,0:T(8,128)} custom-call(s32[256]{0:T(256)S(1)} %bitcast.83, bf16[3,64,16,128]{3,2,1,0:T(8,128)(2,1)S(1)} %copy-done.19, bf16[192,16,128]{2,1,0:T(8,128)(2,1)S(1)} %copy-done.22, bf16[64,128,128]{2,1,0:T(8,128)(2,1)S(1)} %copy-done, bf16[4,256,384]{2,1,0:T(8,128)(2,1)S(1)} %copy-done.14, ...), custom_call_target="tpu_custom_call" | custom-call | flops 7381975040 | bytes 16777216 | tf_op jit(solution)/shard_map/pallas_call | solution.py:159
  164.6 7.7 %shard_map.79.refs_5_ = f32[1024,1024]{1,0:T(8,128)S(1)} custom-call(s32[256]{0:T(256)S(1)} %bitcast.75, bf16[3,64,16,128]{3,2,1,0:T(8,128)(2,1)S(1)} %copy-done.13, bf16[192,16,128]{2,1,0:T(8,128)(2,1)} %collective-permute-done.23.refs_2_, bf16[64,128,128]{2,1,0:T(8,128)(2,1)S(1)} %copy-done, bf16[4,256,384]{2,1,0:T(8,128)(2,1)S(1)} %get-tuple-element.102.refs_4_, ...), custom_call_target="tpu_custom_call" | custom-call | flops 939524096 | bytes 16777216 | tf_op jit(solution)/shard_map/pallas_call | solution.py:159
  174.2 4.2 %collective-permute-done.22.refs_2_ = bf16[192,16,128]{2,1,0:T(8,128)(2,1)} collective-permute-done((bf16[192,16,128]{2,1,0:T(8,128)(2,1)}, bf16[192,16,128]{2,1,0:T(8,128)(2,1)}, u32[]{:S(2)}, u32[]{:S(2)}) %collective-permute-start.22) | collective-permute-done | bytes 786464 | tf_op jit(solution)/shard_map/ppermute | solution.py:266
  178.5 7.5 %shard_map.81.refs_5_ = f32[1024,1024]{1,0:T(8,128)S(1)} custom-call(s32[256]{0:T(256)S(1)} %bitcast.79, bf16[3,64,16,128]{3,2,1,0:T(8,128)(2,1)S(1)} %copy-done.11, bf16[192,16,128]{2,1,0:T(8,128)(2,1)} %collective-permute-done.22.refs_2_, bf16[64,128,128]{2,1,0:T(8,128)(2,1)S(1)} %copy-done, bf16[4,256,384]{2,1,0:T(8,128)(2,1)S(1)} %get-tuple-element.103.refs_4_, ...), custom_call_target="tpu_custom_call" | custom-call | flops 939524096 | bytes 16777216 | tf_op jit(solution)/shard_map/pallas_call | solution.py:159
  186.1 9.3 %collective-permute-done.25.refs_2_ = bf16[192,16,128]{2,1,0:T(8,128)(2,1)} collective-permute-done((bf16[192,16,128]{2,1,0:T(8,128)(2,1)}, bf16[192,16,128]{2,1,0:T(8,128)(2,1)}, u32[]{:S(2)}, u32[]{:S(2)}) %collective-permute-start.25) | collective-permute-done | bytes 786464 | tf_op jit(solution)/shard_map/ppermute | solution.py:266
  195.3 15.2 %collective-permute-done.24.refs_2_ = bf16[192,16,128]{2,1,0:T(8,128)(2,1)S(1)} collective-permute-done((bf16[192,16,128]{2,1,0:T(8,128)(2,1)}, bf16[192,16,128]{2,1,0:T(8,128)(2,1)S(1)}, u32[]{:S(2)}, u32[]{:S(2)}) %collective-permute-start.24) | collective-permute-done | bytes 786464 | tf_op jit(solution)/shard_map/ppermute | solution.py:266
  210.6 6.9 %shard_map.82.refs_5_ = f32[1024,1024]{1,0:T(8,128)S(1)} custom-call(s32[256]{0:T(256)S(1)} %bitcast.76, bf16[3,64,16,128]{3,2,1,0:T(8,128)(2,1)S(1)} %copy-done.13, bf16[192,16,128]{2,1,0:T(8,128)(2,1)S(1)} %collective-permute-done.24.refs_2_, bf16[64,128,128]{2,1,0:T(8,128)(2,1)S(1)} %copy-done, bf16[4,256,384]{2,1,0:T(8,128)(2,1)S(1)} %get-tuple-element.102.refs_4_, ...), custom_call_target="tpu_custom_call" | custom-call | flops 939524096 | bytes 16777216 | tf_op jit(solution)/shard_map/pallas_call | solution.py:159
  217.5 15.1 %shard_map.83.refs_8_ = f32[2,24,128,512]{3,2,1,0:T(8,128)} custom-call(s32[256]{0:T(256)S(1)} %bitcast.84, bf16[3,64,16,128]{3,2,1,0:T(8,128)(2,1)S(1)} %copy-done.20, bf16[192,16,128]{2,1,0:T(8,128)(2,1)} %collective-permute-done.25.refs_2_, bf16[64,128,128]{2,1,0:T(8,128)(2,1)S(1)} %copy-done, ...), custom_call_target="tpu_custom_call", output_to_operand_aliasing={{}: (8, {})} | custom-call | flops 7381975040 | bytes 16777216 | tf_op jit(solution)/shard_map/pallas_call | solution.py:159
  232.7 14.5 %shard_map.84 = f32[2,24,128,512]{3,2,1,0:T(8,128)} custom-call(s32[256]{0:T(256)S(1)} %bitcast.85, bf16[3,64,16,128]{3,2,1,0:T(8,128)(2,1)S(1)} %copy-done.20, bf16[192,16,128]{2,1,0:T(8,128)(2,1)S(1)} %collective-permute-done.26.refs_2_, bf16[64,128,128]{2,1,0:T(8,128)(2,1)S(1)} %copy-done, ...), custom_call_target="tpu_custom_call", output_to_operand_aliasing={{}: (8, {})} | custom-call | flops 7381975040 | bytes 16777216 | tf_op jit(solution)/shard_map/pallas_call | solution.py:159
  (113 shorter events, 34.0 us)
Async XLA Ops:
  1.4 6.3 %collective-permute-start.2 = (s32[2,64]{1,0:T(2,128)S(1)}, s32[2,64]{1,0:T(2,128)S(1)}, u32[]{:S(2)}, u32[]{:S(2)}) collective-permute-start(s32[2,64]{1,0:T(2,128)S(1)} %get-tuple-element.122), channel_id=1, source_target_pairs={{0,24},{8,0},{16,8},{24,16},{1,25},{9,1},{17,9},{25,17},{2,26},{10... | collective-permute-start | bytes 1544 | tf_op jit(solution)/shard_map/ppermute | solution.py:191
  6.4 4.5 %collective-permute-start.1 = (s32[2,64]{1,0:T(2,128)S(1)}, s32[2,64]{1,0:T(2,128)S(1)}, u32[]{:S(2)}, u32[]{:S(2)}) collective-permute-start(s32[2,64]{1,0:T(2,128)S(1)} %get-tuple-element.122), channel_id=1, source_target_pairs={{0,16},{8,24},{16,0},{24,8},{1,17},{9,25},{17,1},{25,9},{2,18},{10... | collective-permute-start | bytes 1544 | tf_op jit(solution)/shard_map/ppermute | solution.py:191
  6.4 5.4 %collective-permute-start = (s32[2,64]{1,0:T(2,128)S(1)}, s32[2,64]{1,0:T(2,128)S(1)}, u32[]{:S(2)}, u32[]{:S(2)}) collective-permute-start(s32[2,64]{1,0:T(2,128)S(1)} %get-tuple-element.122), channel_id=1, source_target_pairs={{0,8},{8,16},{16,24},{24,0},{1,9},{9,17},{17,25},{25,1},{2,10},{10... | collective-permute-start | bytes 1544 | tf_op jit(solution)/shard_map/ppermute | solution.py:191
  11.8 11.7 %collective-permute-start.5 = (s32[4,2,64]{2,1,0:T(2,128)S(1)}, s32[4,2,64]{2,1,0:T(2,128)S(1)}, u32[]{:S(2)}, u32[]{:S(2)}) collective-permute-start(s32[4,2,64]{2,1,0:T(2,128)S(1)} %pad_add_fusion), channel_id=1, source_target_pairs={{0,3},{1,2},{2,1},{3,0},{4,7},{5,6},{6,5},{7,4},{8,11},{9,10},{10,... | collective-permute-start | bytes 6152 | tf_op jit(solution)/shard_map/ppermute | solution.py:194
  14.2 9.8 %collective-permute-start.4 = (s32[4,2,64]{2,1,0:T(2,128)S(1)}, s32[4,2,64]{2,1,0:T(2,128)S(1)}, u32[]{:S(2)}, u32[]{:S(2)}) collective-permute-start(s32[4,2,64]{2,1,0:T(2,128)S(1)} %pad_add_fusion), channel_id=1, source_target_pairs={{0,2},{1,3},{2,0},{3,1},{4,6},{5,7},{6,4},{7,5},{8,10},{9,11},{10,... | collective-permute-start | bytes 6152 | tf_op jit(solution)/shard_map/ppermute | solution.py:194
  14.7 9.3 %collective-permute-start.3 = (s32[4,2,64]{2,1,0:T(2,128)S(1)}, s32[4,2,64]{2,1,0:T(2,128)S(1)}, u32[]{:S(2)}, u32[]{:S(2)}) collective-permute-start(s32[4,2,64]{2,1,0:T(2,128)S(1)} %pad_add_fusion), channel_id=1, source_target_pairs={{0,1},{1,0},{2,3},{3,2},{4,5},{5,4},{6,7},{7,6},{8,9},{9,8},{10,11... | collective-permute-start | bytes 6152 | tf_op jit(solution)/shard_map/ppermute | solution.py:194
  19.6 28.9 %copy-start.5 = (bf16[3,64,16,128]{3,2,1,0:T(8,128)(2,1)}, bf16[3,64,16,128]{3,2,1,0:T(8,128)(2,1)S(1)}, u32[]{:S(2)}) copy-start(bf16[3,64,16,128]{3,2,1,0:T(8,128)(2,1)S(1)} %get-tuple-element.107.refs_1_) | copy-start | bytes 2359300
  20.5 10.4 %collective-permute-start.8 = (bf16[64,16,128]{2,1,0:T(8,128)(2,1)}, bf16[64,16,128]{2,1,0:T(8,128)(2,1)}, u32[]{:S(2)}, u32[]{:S(2)}) collective-permute-start(bf16[64,16,128]{2,1,0:T(8,128)(2,1)} %get-tuple-element.112), channel_id=1, source_target_pairs={{0,3},{1,2},{2,1},{3,0},{4,7},{5,6},{6,5},{7,4},{8,11},{9,10},{10,... | collective-permute-start | bytes 786440 | tf_op jit(solution)/shard_map/ppermute | solution.py:194
  23.0 10.2 %collective-permute-start.7 = (bf16[64,16,128]{2,1,0:T(8,128)(2,1)}, bf16[64,16,128]{2,1,0:T(8,128)(2,1)}, u32[]{:S(2)}, u32[]{:S(2)}) collective-permute-start(bf16[64,16,128]{2,1,0:T(8,128)(2,1)} %get-tuple-element.113), channel_id=1, source_target_pairs={{0,2},{1,3},{2,0},{3,1},{4,6},{5,7},{6,4},{7,5},{8,10},{9,11},{10,... | collective-permute-start | bytes 786440 | tf_op jit(solution)/shard_map/ppermute | solution.py:194
  23.5 9.8 %collective-permute-start.6 = (bf16[64,16,128]{2,1,0:T(8,128)(2,1)}, bf16[64,16,128]{2,1,0:T(8,128)(2,1)}, u32[]{:S(2)}, u32[]{:S(2)}) collective-permute-start(bf16[64,16,128]{2,1,0:T(8,128)(2,1)} %get-tuple-element.111), channel_id=1, source_target_pairs={{0,1},{1,0},{2,3},{3,2},{4,5},{5,4},{6,7},{7,6},{8,9},{9,8},{10,11... | collective-permute-start | bytes 786440 | tf_op jit(solution)/shard_map/ppermute | solution.py:194
  24.0 19.5 %collective-permute-start.14 = (bf16[3,64,16,128]{3,2,1,0:T(8,128)(2,1)S(1)}, bf16[3,64,16,128]{3,2,1,0:T(8,128)(2,1)S(1)}, u32[]{:S(2)}, u32[]{:S(2)}) collective-permute-start(bf16[3,64,16,128]{3,2,1,0:T(8,128)(2,1)S(1)} %get-tuple-element.107.refs_1_), channel_id=1, source_target_pairs={{0,8},{8,16},{16,24},{24,0},{1,9},{9,17},{17,25},{25,1},{2,10},{10... | collective-permute-start | bytes 2359304 | tf_op jit(solution)/shard_map/ppermute | solution.py:266
  35.4 41.8 %collective-permute-start.11 = (bf16[64,16,128]{2,1,0:T(8,128)(2,1)S(1)}, bf16[64,16,128]{2,1,0:T(8,128)(2,1)S(1)}, u32[]{:S(2)}, u32[]{:S(2)}) collective-permute-start(bf16[64,16,128]{2,1,0:T(8,128)(2,1)S(1)} %slice_bitcast_fusion.7), channel_id=1, source_target_pairs={{0,3},{1,2},{2,1},{3,0},{4,7},{5,6},{6,5},{7,4},{8,11},{9,10},{10,... | collective-permute-start | bytes 786440 | tf_op jit(solution)/shard_map/ppermute | solution.py:194
  37.1 23.2 %collective-permute-start.12 = (bf16[192,16,128]{2,1,0:T(8,128)(2,1)S(1)}, bf16[192,16,128]{2,1,0:T(8,128)(2,1)S(1)}, u32[]{:S(2)}, u32[]{:S(2)}) collective-permute-start(bf16[192,16,128]{2,1,0:T(8,128)(2,1)S(1)} %pad_maximum_fusion.1.refs_2_), channel_id=1, source_target_pairs={{0,8},{8,16},{16,24},{24,0},{1,9},{9,17},{17,25},{25,1},{2,10},{10... | collective-permute-start | bytes 2359304 | tf_op jit(solution)/shard_map/ppermute | solution.py:266
  43.5 33.7 %collective-permute-start.15 = (bf16[3,64,16,128]{3,2,1,0:T(8,128)(2,1)S(1)}, bf16[3,64,16,128]{3,2,1,0:T(8,128)(2,1)S(1)}, u32[]{:S(2)}, u32[]{:S(2)}) collective-permute-start(bf16[3,64,16,128]{3,2,1,0:T(8,128)(2,1)S(1)} %collective-permute-done.14.refs_1_), channel_id=1, source_target_pairs={{0,8},{8,16},{16,24},{24,0},{1,9},{9,17},{17,25},{25,1},{2,10},{10... | collective-permute-start | bytes 2359304 | tf_op jit(solution)/shard_map/ppermute | solution.py:266
  43.6 33.7 %collective-permute-start.10 = (bf16[64,16,128]{2,1,0:T(8,128)(2,1)S(1)}, bf16[64,16,128]{2,1,0:T(8,128)(2,1)S(1)}, u32[]{:S(2)}, u32[]{:S(2)}) collective-permute-start(bf16[64,16,128]{2,1,0:T(8,128)(2,1)S(1)} %slice_bitcast_fusion.8), channel_id=1, source_target_pairs={{0,2},{1,3},{2,0},{3,1},{4,6},{5,7},{6,4},{7,5},{8,10},{9,11},{10,... | collective-permute-start | bytes 786440 | tf_op jit(solution)/shard_map/ppermute | solution.py:194
  45.5 31.7 %collective-permute-start.9 = (bf16[64,16,128]{2,1,0:T(8,128)(2,1)S(1)}, bf16[64,16,128]{2,1,0:T(8,128)(2,1)S(1)}, u32[]{:S(2)}, u32[]{:S(2)}) collective-permute-start(bf16[64,16,128]{2,1,0:T(8,128)(2,1)S(1)} %slice_bitcast_fusion.9), channel_id=1, source_target_pairs={{0,1},{1,0},{2,3},{3,2},{4,5},{5,4},{6,7},{7,6},{8,9},{9,8},{10,11... | collective-permute-start | bytes 786440 | tf_op jit(solution)/shard_map/ppermute | solution.py:194
  60.4 33.7 %collective-permute-start.13 = (bf16[192,16,128]{2,1,0:T(8,128)(2,1)S(1)}, bf16[192,16,128]{2,1,0:T(8,128)(2,1)S(1)}, u32[]{:S(2)}, u32[]{:S(2)}) collective-permute-start(bf16[192,16,128]{2,1,0:T(8,128)(2,1)S(1)} %collective-permute-done.12.refs_2_), channel_id=1, source_target_pairs={{0,8},{8,16},{16,24},{24,0},{1,9},{9,17},{17,25},{25,1},{2,10},{10... | collective-permute-start | bytes 2359304 | tf_op jit(solution)/shard_map/ppermute | solution.py:266
  77.2 33.7 %collective-permute-start.16 = (bf16[3,64,16,128]{3,2,1,0:T(8,128)(2,1)S(1)}, bf16[3,64,16,128]{3,2,1,0:T(8,128)(2,1)S(1)}, u32[]{:S(2)}, u32[]{:S(2)}) collective-permute-start(bf16[3,64,16,128]{3,2,1,0:T(8,128)(2,1)S(1)} %collective-permute-done.15.refs_1_), channel_id=1, source_target_pairs={{0,8},{8,16},{16,24},{24,0},{1,9},{9,17},{17,25},{25,1},{2,10},{10... | collective-permute-start | bytes 2359304 | tf_op jit(solution)/shard_map/ppermute | solution.py:266
  77.4 39.0 %collective-permute-start.17 = (bf16[64,16,128]{2,1,0:T(8,128)(2,1)S(1)}, bf16[64,16,128]{2,1,0:T(8,128)(2,1)S(1)}, u32[]{:S(2)}, u32[]{:S(2)}) collective-permute-start(bf16[64,16,128]{2,1,0:T(8,128)(2,1)S(1)} %slice_bitcast_fusion.6), channel_id=1, source_target_pairs={{0,1},{1,0},{2,3},{3,2},{4,5},{5,4},{6,7},{7,6},{8,9},{9,8},{10,11... | collective-permute-start | bytes 786440 | tf_op jit(solution)/shard_map/ppermute | solution.py:194
  79.2 37.9 %collective-permute-start.18 = (bf16[64,16,128]{2,1,0:T(8,128)(2,1)S(1)}, bf16[64,16,128]{2,1,0:T(8,128)(2,1)S(1)}, u32[]{:S(2)}, u32[]{:S(2)}) collective-permute-start(bf16[64,16,128]{2,1,0:T(8,128)(2,1)S(1)} %slice_bitcast_fusion.5), channel_id=1, source_target_pairs={{0,2},{1,3},{2,0},{3,1},{4,6},{5,7},{6,4},{7,5},{8,10},{9,11},{10,... | collective-permute-start | bytes 786440 | tf_op jit(solution)/shard_map/ppermute | solution.py:194
  94.1 37.0 %collective-permute-start.21 = (bf16[192,16,128]{2,1,0:T(8,128)(2,1)S(1)}, bf16[192,16,128]{2,1,0:T(8,128)(2,1)}, u32[]{:S(2)}, u32[]{:S(2)}) collective-permute-start(bf16[192,16,128]{2,1,0:T(8,128)(2,1)S(1)} %pad_maximum_fusion.2.refs_2_), channel_id=1, source_target_pairs={{0,8},{8,16},{16,24},{24,0},{1,9},{9,17},{17,25},{25,1},{2,10},{10... | collective-permute-start | bytes 2359304 | tf_op jit(solution)/shard_map/ppermute | solution.py:266
  111.0 33.7 %collective-permute-start.20 = (bf16[192,16,128]{2,1,0:T(8,128)(2,1)S(1)}, bf16[192,16,128]{2,1,0:T(8,128)(2,1)S(1)}, u32[]{:S(2)}, u32[]{:S(2)}) collective-permute-start(bf16[192,16,128]{2,1,0:T(8,128)(2,1)S(1)} %collective-permute-done.13.refs_2_), channel_id=1, source_target_pairs={{0,8},{8,16},{16,24},{24,0},{1,9},{9,17},{17,25},{25,1},{2,10},{10... | collective-permute-start | bytes 2359304 | tf_op jit(solution)/shard_map/ppermute | solution.py:266
  112.1 8.7 %collective-permute-start.19 = (bf16[64,16,128]{2,1,0:T(8,128)(2,1)S(1)}, bf16[64,16,128]{2,1,0:T(8,128)(2,1)S(1)}, u32[]{:S(2)}, u32[]{:S(2)}) collective-permute-start(bf16[64,16,128]{2,1,0:T(8,128)(2,1)S(1)} %slice_bitcast_fusion.4), channel_id=1, source_target_pairs={{0,3},{1,2},{2,1},{3,0},{4,7},{5,6},{6,5},{7,4},{8,11},{9,10},{10,... | collective-permute-start | bytes 786440 | tf_op jit(solution)/shard_map/ppermute | solution.py:194
  131.1 33.5 %collective-permute-start.23 = (bf16[192,16,128]{2,1,0:T(8,128)(2,1)}, bf16[192,16,128]{2,1,0:T(8,128)(2,1)}, u32[]{:S(2)}, u32[]{:S(2)}) collective-permute-start(bf16[192,16,128]{2,1,0:T(8,128)(2,1)} %collective-permute-done.21.refs_2_), channel_id=1, source_target_pairs={{0,8},{8,16},{16,24},{24,0},{1,9},{9,17},{17,25},{25,1},{2,10},{10... | collective-permute-start | bytes 2359304 | tf_op jit(solution)/shard_map/ppermute | solution.py:266
  145.5 32.9 %collective-permute-start.22 = (bf16[192,16,128]{2,1,0:T(8,128)(2,1)}, bf16[192,16,128]{2,1,0:T(8,128)(2,1)}, u32[]{:S(2)}, u32[]{:S(2)}) collective-permute-start(bf16[192,16,128]{2,1,0:T(8,128)(2,1)} %constant_dynamic-update-slice_fusion.refs_2_), channel_id=1, source_target_pairs={{0,8},{8,16},{16,24},{24,0},{1,9},{9,17},{17,25},{25,1},{2,10},{10... | collective-permute-start | bytes 2359304 | tf_op jit(solution)/shard_map/ppermute | solution.py:266
  164.5 30.8 %collective-permute-start.25 = (bf16[192,16,128]{2,1,0:T(8,128)(2,1)}, bf16[192,16,128]{2,1,0:T(8,128)(2,1)}, u32[]{:S(2)}, u32[]{:S(2)}) collective-permute-start(bf16[192,16,128]{2,1,0:T(8,128)(2,1)} %collective-permute-done.23.refs_2_), channel_id=1, source_target_pairs={{0,8},{8,16},{16,24},{24,0},{1,9},{9,17},{17,25},{25,1},{2,10},{10... | collective-permute-start | bytes 2359304 | tf_op jit(solution)/shard_map/ppermute | solution.py:266
  178.5 32.1 %collective-permute-start.24 = (bf16[192,16,128]{2,1,0:T(8,128)(2,1)}, bf16[192,16,128]{2,1,0:T(8,128)(2,1)S(1)}, u32[]{:S(2)}, u32[]{:S(2)}) collective-permute-start(bf16[192,16,128]{2,1,0:T(8,128)(2,1)} %collective-permute-done.22.refs_2_), channel_id=1, source_target_pairs={{0,8},{8,16},{16,24},{24,0},{1,9},{9,17},{17,25},{25,1},{2,10},{10... | collective-permute-start | bytes 2359304 | tf_op jit(solution)/shard_map/ppermute | solution.py:266
  186.0 31.5 %copy-start.4 = (f32[1024,1024]{1,0:T(8,128)S(1)}, f32[1024,1024]{1,0:T(8,128)}, u32[]{:S(2)}) copy-start(f32[1024,1024]{1,0:T(8,128)} %copy-done.3) | copy-start | bytes 12582916
  186.0 31.5 %copy-start.8 = (bf16[1024,1024]{1,0:T(8,128)(2,1)S(1)}, bf16[1024,1024]{1,0:T(8,128)(2,1)}, u32[]{:S(2)}) copy-start(bf16[1024,1024]{1,0:T(8,128)(2,1)} %constant.84.clone.refs_6_) | copy-start | bytes 6291460
  186.0 31.5 %copy-start.15 = (bf16[4,256,384]{2,1,0:T(8,128)(2,1)S(1)}, bf16[4,256,384]{2,1,0:T(8,128)(2,1)}, u32[]{:S(2)}) copy-start(bf16[4,256,384]{2,1,0:T(8,128)(2,1)} %get-tuple-element.101.refs_4_) | copy-start | bytes 2359300
  186.1 31.5 %copy-start.20 = (bf16[3,64,16,128]{3,2,1,0:T(8,128)(2,1)S(1)}, bf16[3,64,16,128]{3,2,1,0:T(8,128)(2,1)}, u32[]{:S(2)}) copy-start(bf16[3,64,16,128]{3,2,1,0:T(8,128)(2,1)} %copy-done.18) | copy-start | bytes 2359300
  210.5 22.1 %collective-permute-start.26 = (bf16[192,16,128]{2,1,0:T(8,128)(2,1)S(1)}, bf16[192,16,128]{2,1,0:T(8,128)(2,1)S(1)}, u32[]{:S(2)}, u32[]{:S(2)}) collective-permute-start(bf16[192,16,128]{2,1,0:T(8,128)(2,1)S(1)} %collective-permute-done.24.refs_2_), channel_id=1, source_target_pairs={{0,8},{8,16},{16,24},{24,0},{1,9},{9,17},{17,25},{25,1},{2,10},{10... | collective-permute-start | bytes 2359304 | tf_op jit(solution)/shard_map/ppermute | solution.py:266
  (20 other events, 207.2 us)

commit v3 on v2

--- a/solution.py
+++ b/solution.py
@@ -251,9 +251,10 @@
             _, m, ahead = order[at - 2]
             send, streams[m][ahead] = lax.optimization_barrier((send, streams[m][ahead]))
         for chunk in range(chunks if at >= 3 else 0):
+            final = at == len(order) - 1
             step_of = taken[chunk]
             if step_of == n_slab or any(
-                place.get((k, step_of), 0) > at - 3 for k in (0, chunk + 1)
+                place.get((k, step_of), 0) > at - (2 if final else 3) for k in (0, chunk + 1)
             ):
                 continue
             value = work(chunk, out)
@@ -262,7 +263,8 @@
                 out = value
             else:
                 total[chunk] = value
-            break
+            if not final:
+                break
         streams[n].append(lax.ppermute(send, "slab", ring))
     for chunk in range(chunks):
         while taken[chunk] < n_slab:

time: 248 us -> 257 us (1.036)
  waiting for transfers between devices: 77.8 us -> 89.4 us
  starting transfers between devices: 29.3 us -> 26.3 us
    ppermute x12, waiting for transfers between devices: 68.2 us -> 80.7 us  [per_device(): streams[n].append(lax.ppermute(send, 'slab', ring))]
    ppermute x12, starting transfers between devices: 22.9 us -> 17.3 us  [swap(): return lax.ppermute(array, 'img', [(i, i ^ k) for i in range(n_img)])]
    ppermute x3, waiting for transfers between devices: 4.35 us -> 1.54 us  [shift(): lax.ppermute(array, 'slab', [(i, (i + step) % n_slab) for i in range(n_sl...]
  transfers between devices with their start and end apart: 27 -> 27, of which waited for: 15 -> 14; matrix products, arithmetic and copies ran while one was open for 7% -> 7% of each run, Pallas kernels for 38% -> 31%
where the time goes in v3:
time: 257 us
  Pallas kernels  110 us (43%)
  waiting for transfers between devices  89.4 us (35%)
  starting transfers between devices  26.3 us (10%)
  local copies, waits for them, and re-layouts  22.6 us (9%)
  other arithmetic  7.85 us (3%)
    pallas_call x12, Pallas kernels, run_chunk(): pl.pallas_call(functools.partial(chunk_kernel, first, last, y_blocks, z_l...  110 us
    ppermute x12, waiting for transfers between devices, per_device(): streams[n].append(lax.ppermute(send, 'slab', ring))  80.7 us
    ppermute x12, starting transfers between devices, swap(): return lax.ppermute(array, 'img', [(i, i ^ k) for i in range(n_img)])  17.3 us
    unnamed x52, local copies, waits for them, and re-layouts  12.8 us
    ppermute x3, starting transfers between devices, shift(): lax.ppermute(array, 'slab', [(i, (i + step) % n_slab) for i in range(n_sl...  7.86 us
    ppermute x12, waiting for transfers between devices, swap(): return lax.ppermute(array, 'img', [(i, i ^ k) for i in range(n_img)])  7.14 us
  transfers between devices with their start and end apart: 27, of which 14 were waited for; matrix products, arithmetic and copies ran while one was open for 7% of the time, Pallas kernels for 31%

profile of v3, /device:TPU:0, one launch (start us, length us, event | category | flops | bytes accessed | tf_op | source)
XLA Modules:
  0.0 256.6 jit_solution(8380893816904213636)
XLA Ops:
  1.4 4.0 %collective-permute-start.1 = (s32[2,64]{1,0:T(2,128)S(1)}, s32[2,64]{1,0:T(2,128)S(1)}, u32[]{:S(2)}, u32[]{:S(2)}) collective-permute-start(s32[2,64]{1,0:T(2,128)S(1)} %get-tuple-element.126), channel_id=1, source_target_pairs={{0,16},{8,24},{16,0},{24,8},{1,17},{9,25},{17,1},{25,9},{2,18},{10... | collective-permute-start | bytes 1544 | tf_op jit(solution)/shard_map/ppermute | solution.py:191
  7.0 2.2 collective-permute-start.2
  10.8 2.5 collective-permute-start.5
  14.3 2.6 %copy.15 = bf16[64,2,4,3,8,128]{5,4,1,0,3,2:T(8,128)(2,1)S(1)} copy(bf16[64,2,4,3,8,128]{5,4,3,2,1,0:T(8,128)(2,1)} %bitcast.88) | data formatting | bytes 6291456 | tf_op jit(solution)/shard_map/reshape | solution.py:215
  23.5 4.2 %fusion.6 = (f32[4,4,128,64]{3,2,1,0:T(8,128)S(1)}, f32[4,4,128,64]{3,2,1,0:T(8,128)S(1)}, f32[4,4,128,64]{3,2,1,0:T(8,128)S(1)}) fusion(s32[4,4,64]{2,1,0:T(4,128)S(1)} %copy.13, s32[128]{0:T(128)S(1)} %iota_add_fusion), kind=kLoop, calls=%fused_computation.26 | loop fusion | flops 1966080 | bytes 1577472 | tf_op jit(solution)/shard_map/neg | solution.py:207
  30.0 2.4 collective-permute-done.8
  37.4 8.0 %collective-permute-done.14.refs_1_ = bf16[3,64,16,128]{3,2,1,0:T(8,128)(2,1)S(1)} collective-permute-done((bf16[3,64,16,128]{3,2,1,0:T(8,128)(2,1)S(1)}, bf16[3,64,16,128]{3,2,1,0:T(8,128)(2,1)S(1)}, u32[]{:S(2)}, u32[]{:S(2)}) %collective-permute-start.14) | collective-permute-done | bytes 786464 | tf_op jit(solution)/shard_map/ppermute | solution.py:268
  48.6 6.9 %shard_map.73.refs_5_ = f32[1024,1024]{1,0:T(8,128)S(1)} custom-call(s32[256]{0:T(256)S(1)} %bitcast.80, bf16[3,64,16,128]{3,2,1,0:T(8,128)(2,1)S(1)} %get-tuple-element.111.refs_1_, bf16[192,16,128]{2,1,0:T(8,128)(2,1)S(1)} %pad_maximum_fusion.1.refs_2_, bf16[64,128,128]{2,1,0:T(8,128)(2,1)S(1)} %copy-done, bf16[4,256,384]{2,1,0:T(8,128)(2,1)S(1)} %get-tuple-element.108.refs_4_), custom_call_target="tpu_custom_call" | custom-call | flops 939524096 | bytes 16777216 | tf_op jit(solution)/shard_map/pallas_call | solution.py:159
  55.5 6.7 %collective-permute-done.12.refs_2_ = bf16[192,16,128]{2,1,0:T(8,128)(2,1)S(1)} collective-permute-done((bf16[192,16,128]{2,1,0:T(8,128)(2,1)S(1)}, bf16[192,16,128]{2,1,0:T(8,128)(2,1)S(1)}, u32[]{:S(2)}, u32[]{:S(2)}) %collective-permute-start.12) | collective-permute-done | bytes 786464 | tf_op jit(solution)/shard_map/ppermute | solution.py:268
  62.2 6.9 %shard_map.74.refs_5_ = f32[1024,1024]{1,0:T(8,128)S(1)} custom-call(s32[256]{0:T(256)S(1)} %bitcast.77, bf16[3,64,16,128]{3,2,1,0:T(8,128)(2,1)S(1)} %collective-permute-done.14.refs_1_, bf16[192,16,128]{2,1,0:T(8,128)(2,1)S(1)} %collective-permute-done.12.refs_2_, bf16[64,128,128]{2,1,0:T(8,128)(2,1)S(1)} %copy-done, ...), custom_call_target="tpu_custom_call" | custom-call | flops 939524096 | bytes 16777216 | tf_op jit(solution)/shard_map/pallas_call | solution.py:159
  69.2 9.9 %collective-permute-done.15.refs_1_ = bf16[3,64,16,128]{3,2,1,0:T(8,128)(2,1)S(1)} collective-permute-done((bf16[3,64,16,128]{3,2,1,0:T(8,128)(2,1)S(1)}, bf16[3,64,16,128]{3,2,1,0:T(8,128)(2,1)S(1)}, u32[]{:S(2)}, u32[]{:S(2)}) %collective-permute-start.15) | collective-permute-done | bytes 786464 | tf_op jit(solution)/shard_map/ppermute | solution.py:268
  82.4 6.9 %shard_map.76.refs_5_ = f32[1024,1024]{1,0:T(8,128)S(1)} custom-call(s32[256]{0:T(256)S(1)} %bitcast.81, bf16[3,64,16,128]{3,2,1,0:T(8,128)(2,1)S(1)} %copy-done.6, bf16[192,16,128]{2,1,0:T(8,128)(2,1)S(1)} %pad_maximum_fusion.2.refs_2_, bf16[64,128,128]{2,1,0:T(8,128)(2,1)S(1)} %copy-done, bf16[4,256,384]{2,1,0:T(8,128)(2,1)S(1)} %get-tuple-element.108.refs_4_), custom_call_target="tpu_custom_call" | custom-call | flops 939524096 | bytes 16777216 | tf_op jit(solution)/shard_map/pallas_call | solution.py:159
  89.3 6.6 %collective-permute-done.13.refs_2_ = bf16[192,16,128]{2,1,0:T(8,128)(2,1)S(1)} collective-permute-done((bf16[192,16,128]{2,1,0:T(8,128)(2,1)S(1)}, bf16[192,16,128]{2,1,0:T(8,128)(2,1)S(1)}, u32[]{:S(2)}, u32[]{:S(2)}) %collective-permute-start.13) | collective-permute-done | bytes 786464 | tf_op jit(solution)/shard_map/ppermute | solution.py:268
  95.9 6.9 %shard_map.75.refs_5_ = f32[1024,1024]{1,0:T(8,128)S(1)} custom-call(s32[256]{0:T(256)S(1)} %bitcast.74, bf16[3,64,16,128]{3,2,1,0:T(8,128)(2,1)S(1)} %collective-permute-done.15.refs_1_, bf16[192,16,128]{2,1,0:T(8,128)(2,1)S(1)} %collective-permute-done.13.refs_2_, bf16[64,128,128]{2,1,0:T(8,128)(2,1)S(1)} %copy-done, ...), custom_call_target="tpu_custom_call" | custom-call | flops 939524096 | bytes 16777216 | tf_op jit(solution)/shard_map/pallas_call | solution.py:159
  102.9 2.0 copy-done.16
  104.9 7.9 %collective-permute-done.16.refs_1_ = bf16[3,64,16,128]{3,2,1,0:T(8,128)(2,1)S(1)} collective-permute-done((bf16[3,64,16,128]{3,2,1,0:T(8,128)(2,1)S(1)}, bf16[3,64,16,128]{3,2,1,0:T(8,128)(2,1)S(1)}, u32[]{:S(2)}, u32[]{:S(2)}) %collective-permute-start.16) | collective-permute-done | bytes 786464 | tf_op jit(solution)/shard_map/ppermute | solution.py:268
  113.9 2.5 collective-permute-start.19
  117.9 3.4 %collective-permute-done.19 = bf16[64,16,128]{2,1,0:T(8,128)(2,1)S(1)} collective-permute-done((bf16[64,16,128]{2,1,0:T(8,128)(2,1)S(1)}, bf16[64,16,128]{2,1,0:T(8,128)(2,1)S(1)}, u32[]{:S(2)}, u32[]{:S(2)}) %collective-permute-start.19) | collective-permute-done | bytes 262176 | tf_op jit(solution)/shard_map/ppermute | solution.py:194
  122.0 7.6 %shard_map.78.refs_5_ = f32[1024,1024]{1,0:T(8,128)S(1)} custom-call(s32[256]{0:T(256)S(1)} %bitcast.82, bf16[3,64,16,128]{3,2,1,0:T(8,128)(2,1)S(1)} %copy-done.6, bf16[192,16,128]{2,1,0:T(8,128)(2,1)} %constant_dynamic-update-slice_fusion.refs_2_, bf16[64,128,128]{2,1,0:T(8,128)(2,1)S(1)} %copy-done, bf16[4,256,384]{2,1,0:T(8,128)(2,1)S(1)} %get-tuple-element.108.refs_4_), custom_call_target="tpu_custom_call" | custom-call | flops 939524096 | bytes 16777216 | tf_op jit(solution)/shard_map/pallas_call | solution.py:159
  132.1 7.8 %shard_map.77.refs_5_ = f32[1024,1024]{1,0:T(8,128)S(1)} custom-call(s32[256]{0:T(256)S(1)} %bitcast.78, bf16[3,64,16,128]{3,2,1,0:T(8,128)(2,1)S(1)} %copy-done.11, bf16[192,16,128]{2,1,0:T(8,128)(2,1)} %collective-permute-done.21.refs_2_, bf16[64,128,128]{2,1,0:T(8,128)(2,1)S(1)} %copy-done, bf16[4,256,384]{2,1,0:T(8,128)(2,1)S(1)} %get-tuple-element.107.refs_4_, ...), custom_call_target="tpu_custom_call" | custom-call | flops 939524096 | bytes 16777216 | tf_op jit(solution)/shard_map/pallas_call | solution.py:159
  139.8 6.7 %collective-permute-done.20.refs_2_ = bf16[192,16,128]{2,1,0:T(8,128)(2,1)S(1)} collective-permute-done((bf16[192,16,128]{2,1,0:T(8,128)(2,1)S(1)}, bf16[192,16,128]{2,1,0:T(8,128)(2,1)S(1)}, u32[]{:S(2)}, u32[]{:S(2)}) %collective-permute-start.20) | collective-permute-done | bytes 786464 | tf_op jit(solution)/shard_map/ppermute | solution.py:268
  148.5 2.2 copy-done.17
  151.9 14.5 %shard_map.80.refs_8_ = f32[2,24,128,512]{3,2,1,0:T(8,128)} custom-call(s32[256]{0:T(256)S(1)} %bitcast.83, bf16[3,64,16,128]{3,2,1,0:T(8,128)(2,1)S(1)} %copy-done.19, bf16[192,16,128]{2,1,0:T(8,128)(2,1)S(1)} %copy-done.22, bf16[64,128,128]{2,1,0:T(8,128)(2,1)S(1)} %copy-done, bf16[4,256,384]{2,1,0:T(8,128)(2,1)S(1)} %copy-done.14, ...), custom_call_target="tpu_custom_call" | custom-call | flops 7381975040 | bytes 16777216 | tf_op jit(solution)/shard_map/pallas_call | solution.py:159
  167.0 7.8 %shard_map.79.refs_5_ = f32[1024,1024]{1,0:T(8,128)S(1)} custom-call(s32[256]{0:T(256)S(1)} %bitcast.75, bf16[3,64,16,128]{3,2,1,0:T(8,128)(2,1)S(1)} %copy-done.13, bf16[192,16,128]{2,1,0:T(8,128)(2,1)} %collective-permute-done.23.refs_2_, bf16[64,128,128]{2,1,0:T(8,128)(2,1)S(1)} %copy-done, bf16[4,256,384]{2,1,0:T(8,128)(2,1)S(1)} %get-tuple-element.106.refs_4_, ...), custom_call_target="tpu_custom_call" | custom-call | flops 939524096 | bytes 16777216 | tf_op jit(solution)/shard_map/pallas_call | solution.py:159
  176.8 3.5 %collective-permute-done.22.refs_2_ = bf16[192,16,128]{2,1,0:T(8,128)(2,1)} collective-permute-done((bf16[192,16,128]{2,1,0:T(8,128)(2,1)}, bf16[192,16,128]{2,1,0:T(8,128)(2,1)}, u32[]{:S(2)}, u32[]{:S(2)}) %collective-permute-start.22) | collective-permute-done | bytes 786464 | tf_op jit(solution)/shard_map/ppermute | solution.py:268
  180.3 7.7 %shard_map.82.refs_5_ = f32[1024,1024]{1,0:T(8,128)S(1)} custom-call(s32[256]{0:T(256)S(1)} %bitcast.79, bf16[3,64,16,128]{3,2,1,0:T(8,128)(2,1)S(1)} %copy-done.11, bf16[192,16,128]{2,1,0:T(8,128)(2,1)} %collective-permute-done.22.refs_2_, bf16[64,128,128]{2,1,0:T(8,128)(2,1)S(1)} %copy-done, bf16[4,256,384]{2,1,0:T(8,128)(2,1)S(1)} %get-tuple-element.107.refs_4_, ...), custom_call_target="tpu_custom_call" | custom-call | flops 939524096 | bytes 16777216 | tf_op jit(solution)/shard_map/pallas_call | solution.py:159
  188.0 9.2 %collective-permute-done.25.refs_2_ = bf16[192,16,128]{2,1,0:T(8,128)(2,1)} collective-permute-done((bf16[192,16,128]{2,1,0:T(8,128)(2,1)}, bf16[192,16,128]{2,1,0:T(8,128)(2,1)}, u32[]{:S(2)}, u32[]{:S(2)}) %collective-permute-start.25) | collective-permute-done | bytes 786464 | tf_op jit(solution)/shard_map/ppermute | solution.py:268
  197.2 12.5 %collective-permute-done.24.refs_2_ = bf16[192,16,128]{2,1,0:T(8,128)(2,1)} collective-permute-done((bf16[192,16,128]{2,1,0:T(8,128)(2,1)}, bf16[192,16,128]{2,1,0:T(8,128)(2,1)}, u32[]{:S(2)}, u32[]{:S(2)}) %collective-permute-start.24) | collective-permute-done | bytes 786464 | tf_op jit(solution)/shard_map/ppermute | solution.py:268
  209.7 15.1 %shard_map.81.refs_8_ = f32[2,24,128,512]{3,2,1,0:T(8,128)} custom-call(s32[256]{0:T(256)S(1)} %bitcast.84, bf16[3,64,16,128]{3,2,1,0:T(8,128)(2,1)S(1)} %copy-done.20, bf16[192,16,128]{2,1,0:T(8,128)(2,1)} %collective-permute-done.25.refs_2_, bf16[64,128,128]{2,1,0:T(8,128)(2,1)S(1)} %copy-done, ...), custom_call_target="tpu_custom_call", output_to_operand_aliasing={{}: (8, {})} | custom-call | flops 7381975040 | bytes 16777216 | tf_op jit(solution)/shard_map/pallas_call | solution.py:159
  224.9 7.5 %shard_map.83.refs_5_ = f32[1024,1024]{1,0:T(8,128)S(1)} custom-call(s32[256]{0:T(256)S(1)} %bitcast.76, bf16[3,64,16,128]{3,2,1,0:T(8,128)(2,1)S(1)} %copy-done.13, bf16[192,16,128]{2,1,0:T(8,128)(2,1)} %collective-permute-done.24.refs_2_, bf16[64,128,128]{2,1,0:T(8,128)(2,1)S(1)} %copy-done, bf16[4,256,384]{2,1,0:T(8,128)(2,1)S(1)} %get-tuple-element.106.refs_4_, ...), custom_call_target="tpu_custom_call" | custom-call | flops 939524096 | bytes 16777216 | tf_op jit(solution)/shard_map/pallas_call | solution.py:159
  232.4 9.7 %collective-permute-done.26.refs_2_ = bf16[192,16,128]{2,1,0:T(8,128)(2,1)S(1)} collective-permute-done((bf16[192,16,128]{2,1,0:T(8,128)(2,1)}, bf16[192,16,128]{2,1,0:T(8,128)(2,1)S(1)}, u32[]{:S(2)}, u32[]{:S(2)}) %collective-permute-start.26) | collective-permute-done | bytes 786464 | tf_op jit(solution)/shard_map/ppermute | solution.py:268
  242.1 14.5 %shard_map.84 = f32[2,24,128,512]{3,2,1,0:T(8,128)} custom-call(s32[256]{0:T(256)S(1)} %bitcast.85, bf16[3,64,16,128]{3,2,1,0:T(8,128)(2,1)S(1)} %copy-done.20, bf16[192,16,128]{2,1,0:T(8,128)(2,1)S(1)} %collective-permute-done.26.refs_2_, bf16[64,128,128]{2,1,0:T(8,128)(2,1)S(1)} %copy-done, ...), custom_call_target="tpu_custom_call", output_to_operand_aliasing={{}: (8, {})} | custom-call | flops 7381975040 | bytes 16777216 | tf_op jit(solution)/shard_map/pallas_call | solution.py:159
  (113 shorter events, 37.4 us)
Async XLA Ops:
  1.4 7.9 %collective-permute-start.1 = (s32[2,64]{1,0:T(2,128)S(1)}, s32[2,64]{1,0:T(2,128)S(1)}, u32[]{:S(2)}, u32[]{:S(2)}) collective-permute-start(s32[2,64]{1,0:T(2,128)S(1)} %get-tuple-element.126), channel_id=1, source_target_pairs={{0,16},{8,24},{16,0},{24,8},{1,17},{9,25},{17,1},{25,9},{2,18},{10... | collective-permute-start | bytes 1544 | tf_op jit(solution)/shard_map/ppermute | solution.py:191
  5.4 5.4 %collective-permute-start = (s32[2,64]{1,0:T(2,128)S(1)}, s32[2,64]{1,0:T(2,128)S(1)}, u32[]{:S(2)}, u32[]{:S(2)}) collective-permute-start(s32[2,64]{1,0:T(2,128)S(1)} %get-tuple-element.126), channel_id=1, source_target_pairs={{0,8},{8,16},{16,24},{24,0},{1,9},{9,17},{17,25},{25,1},{2,10},{10... | collective-permute-start | bytes 1544 | tf_op jit(solution)/shard_map/ppermute | solution.py:191
  7.0 3.8 %collective-permute-start.2 = (s32[2,64]{1,0:T(2,128)S(1)}, s32[2,64]{1,0:T(2,128)S(1)}, u32[]{:S(2)}, u32[]{:S(2)}) collective-permute-start(s32[2,64]{1,0:T(2,128)S(1)} %get-tuple-element.126), channel_id=1, source_target_pairs={{0,24},{8,0},{16,8},{24,16},{1,25},{9,1},{17,9},{25,17},{2,26},{10... | collective-permute-start | bytes 1544 | tf_op jit(solution)/shard_map/ppermute | solution.py:191
  10.8 11.8 %collective-permute-start.5 = (s32[4,2,64]{2,1,0:T(2,128)S(1)}, s32[4,2,64]{2,1,0:T(2,128)S(1)}, u32[]{:S(2)}, u32[]{:S(2)}) collective-permute-start(s32[4,2,64]{2,1,0:T(2,128)S(1)} %pad_add_fusion), channel_id=1, source_target_pairs={{0,3},{1,2},{2,1},{3,0},{4,7},{5,6},{6,5},{7,4},{8,11},{9,10},{10,... | collective-permute-start | bytes 6152 | tf_op jit(solution)/shard_map/ppermute | solution.py:194
  13.3 9.8 %collective-permute-start.4 = (s32[4,2,64]{2,1,0:T(2,128)S(1)}, s32[4,2,64]{2,1,0:T(2,128)S(1)}, u32[]{:S(2)}, u32[]{:S(2)}) collective-permute-start(s32[4,2,64]{2,1,0:T(2,128)S(1)} %pad_add_fusion), channel_id=1, source_target_pairs={{0,2},{1,3},{2,0},{3,1},{4,6},{5,7},{6,4},{7,5},{8,10},{9,11},{10,... | collective-permute-start | bytes 6152 | tf_op jit(solution)/shard_map/ppermute | solution.py:194
  13.8 9.3 %collective-permute-start.3 = (s32[4,2,64]{2,1,0:T(2,128)S(1)}, s32[4,2,64]{2,1,0:T(2,128)S(1)}, u32[]{:S(2)}, u32[]{:S(2)}) collective-permute-start(s32[4,2,64]{2,1,0:T(2,128)S(1)} %pad_add_fusion), channel_id=1, source_target_pairs={{0,1},{1,0},{2,3},{3,2},{4,5},{5,4},{6,7},{7,6},{8,9},{9,8},{10,11... | collective-permute-start | bytes 6152 | tf_op jit(solution)/shard_map/ppermute | solution.py:194
  18.7 29.9 %copy-start.5 = (bf16[3,64,16,128]{3,2,1,0:T(8,128)(2,1)}, bf16[3,64,16,128]{3,2,1,0:T(8,128)(2,1)S(1)}, u32[]{:S(2)}) copy-start(bf16[3,64,16,128]{3,2,1,0:T(8,128)(2,1)S(1)} %get-tuple-element.111.refs_1_) | copy-start | bytes 2359300
  19.6 10.4 %collective-permute-start.6 = (bf16[64,16,128]{2,1,0:T(8,128)(2,1)}, bf16[64,16,128]{2,1,0:T(8,128)(2,1)}, u32[]{:S(2)}, u32[]{:S(2)}) collective-permute-start(bf16[64,16,128]{2,1,0:T(8,128)(2,1)} %get-tuple-element.115), channel_id=1, source_target_pairs={{0,1},{1,0},{2,3},{3,2},{4,5},{5,4},{6,7},{7,6},{8,9},{9,8},{10,11... | collective-permute-start | bytes 786440 | tf_op jit(solution)/shard_map/ppermute | solution.py:194
  21.1 11.3 %collective-permute-start.8 = (bf16[64,16,128]{2,1,0:T(8,128)(2,1)}, bf16[64,16,128]{2,1,0:T(8,128)(2,1)}, u32[]{:S(2)}, u32[]{:S(2)}) collective-permute-start(bf16[64,16,128]{2,1,0:T(8,128)(2,1)} %get-tuple-element.116), channel_id=1, source_target_pairs={{0,3},{1,2},{2,1},{3,0},{4,7},{5,6},{6,5},{7,4},{8,11},{9,10},{10,... | collective-permute-start | bytes 786440 | tf_op jit(solution)/shard_map/ppermute | solution.py:194
  22.6 11.2 %collective-permute-start.7 = (bf16[64,16,128]{2,1,0:T(8,128)(2,1)}, bf16[64,16,128]{2,1,0:T(8,128)(2,1)}, u32[]{:S(2)}, u32[]{:S(2)}) collective-permute-start(bf16[64,16,128]{2,1,0:T(8,128)(2,1)} %get-tuple-element.117), channel_id=1, source_target_pairs={{0,2},{1,3},{2,0},{3,1},{4,6},{5,7},{6,4},{7,5},{8,10},{9,11},{10,... | collective-permute-start | bytes 786440 | tf_op jit(solution)/shard_map/ppermute | solution.py:194
  23.1 22.3 %collective-permute-start.14 = (bf16[3,64,16,128]{3,2,1,0:T(8,128)(2,1)S(1)}, bf16[3,64,16,128]{3,2,1,0:T(8,128)(2,1)S(1)}, u32[]{:S(2)}, u32[]{:S(2)}) collective-permute-start(bf16[3,64,16,128]{3,2,1,0:T(8,128)(2,1)S(1)} %get-tuple-element.111.refs_1_), channel_id=1, source_target_pairs={{0,8},{8,16},{16,24},{24,0},{1,9},{9,17},{17,25},{25,1},{2,10},{10... | collective-permute-start | bytes 2359304 | tf_op jit(solution)/shard_map/ppermute | solution.py:268
  35.9 43.2 %collective-permute-start.11 = (bf16[64,16,128]{2,1,0:T(8,128)(2,1)S(1)}, bf16[64,16,128]{2,1,0:T(8,128)(2,1)S(1)}, u32[]{:S(2)}, u32[]{:S(2)}) collective-permute-start(bf16[64,16,128]{2,1,0:T(8,128)(2,1)S(1)} %slice_bitcast_fusion.7), channel_id=1, source_target_pairs={{0,3},{1,2},{2,1},{3,0},{4,7},{5,6},{6,5},{7,4},{8,11},{9,10},{10,... | collective-permute-start | bytes 786440 | tf_op jit(solution)/shard_map/ppermute | solution.py:194
  37.4 24.8 %collective-permute-start.12 = (bf16[192,16,128]{2,1,0:T(8,128)(2,1)S(1)}, bf16[192,16,128]{2,1,0:T(8,128)(2,1)S(1)}, u32[]{:S(2)}, u32[]{:S(2)}) collective-permute-start(bf16[192,16,128]{2,1,0:T(8,128)(2,1)S(1)} %pad_maximum_fusion.1.refs_2_), channel_id=1, source_target_pairs={{0,8},{8,16},{16,24},{24,0},{1,9},{9,17},{17,25},{25,1},{2,10},{10... | collective-permute-start | bytes 2359304 | tf_op jit(solution)/shard_map/ppermute | solution.py:268
  45.4 33.7 %collective-permute-start.15 = (bf16[3,64,16,128]{3,2,1,0:T(8,128)(2,1)S(1)}, bf16[3,64,16,128]{3,2,1,0:T(8,128)(2,1)S(1)}, u32[]{:S(2)}, u32[]{:S(2)}) collective-permute-start(bf16[3,64,16,128]{3,2,1,0:T(8,128)(2,1)S(1)} %collective-permute-done.14.refs_1_), channel_id=1, source_target_pairs={{0,8},{8,16},{16,24},{24,0},{1,9},{9,17},{17,25},{25,1},{2,10},{10... | collective-permute-start | bytes 2359304 | tf_op jit(solution)/shard_map/ppermute | solution.py:268
  45.4 33.7 %collective-permute-start.10 = (bf16[64,16,128]{2,1,0:T(8,128)(2,1)S(1)}, bf16[64,16,128]{2,1,0:T(8,128)(2,1)S(1)}, u32[]{:S(2)}, u32[]{:S(2)}) collective-permute-start(bf16[64,16,128]{2,1,0:T(8,128)(2,1)S(1)} %slice_bitcast_fusion.8), channel_id=1, source_target_pairs={{0,2},{1,3},{2,0},{3,1},{4,6},{5,7},{6,4},{7,5},{8,10},{9,11},{10,... | collective-permute-start | bytes 786440 | tf_op jit(solution)/shard_map/ppermute | solution.py:194
  47.0 32.1 %collective-permute-start.9 = (bf16[64,16,128]{2,1,0:T(8,128)(2,1)S(1)}, bf16[64,16,128]{2,1,0:T(8,128)(2,1)S(1)}, u32[]{:S(2)}, u32[]{:S(2)}) collective-permute-start(bf16[64,16,128]{2,1,0:T(8,128)(2,1)S(1)} %slice_bitcast_fusion.9), channel_id=1, source_target_pairs={{0,1},{1,0},{2,3},{3,2},{4,5},{5,4},{6,7},{7,6},{8,9},{9,8},{10,11... | collective-permute-start | bytes 786440 | tf_op jit(solution)/shard_map/ppermute | solution.py:194
  62.2 33.7 %collective-permute-start.13 = (bf16[192,16,128]{2,1,0:T(8,128)(2,1)S(1)}, bf16[192,16,128]{2,1,0:T(8,128)(2,1)S(1)}, u32[]{:S(2)}, u32[]{:S(2)}) collective-permute-start(bf16[192,16,128]{2,1,0:T(8,128)(2,1)S(1)} %collective-permute-done.12.refs_2_), channel_id=1, source_target_pairs={{0,8},{8,16},{16,24},{24,0},{1,9},{9,17},{17,25},{25,1},{2,10},{10... | collective-permute-start | bytes 2359304 | tf_op jit(solution)/shard_map/ppermute | solution.py:268
  79.1 33.7 %collective-permute-start.16 = (bf16[3,64,16,128]{3,2,1,0:T(8,128)(2,1)S(1)}, bf16[3,64,16,128]{3,2,1,0:T(8,128)(2,1)S(1)}, u32[]{:S(2)}, u32[]{:S(2)}) collective-permute-start(bf16[3,64,16,128]{3,2,1,0:T(8,128)(2,1)S(1)} %collective-permute-done.15.refs_1_), channel_id=1, source_target_pairs={{0,8},{8,16},{16,24},{24,0},{1,9},{9,17},{17,25},{25,1},{2,10},{10... | collective-permute-start | bytes 2359304 | tf_op jit(solution)/shard_map/ppermute | solution.py:268
  79.2 37.9 %collective-permute-start.18 = (bf16[64,16,128]{2,1,0:T(8,128)(2,1)S(1)}, bf16[64,16,128]{2,1,0:T(8,128)(2,1)S(1)}, u32[]{:S(2)}, u32[]{:S(2)}) collective-permute-start(bf16[64,16,128]{2,1,0:T(8,128)(2,1)S(1)} %slice_bitcast_fusion.5), channel_id=1, source_target_pairs={{0,2},{1,3},{2,0},{3,1},{4,6},{5,7},{6,4},{7,5},{8,10},{9,11},{10,... | collective-permute-start | bytes 786440 | tf_op jit(solution)/shard_map/ppermute | solution.py:194
  80.8 35.6 %collective-permute-start.17 = (bf16[64,16,128]{2,1,0:T(8,128)(2,1)S(1)}, bf16[64,16,128]{2,1,0:T(8,128)(2,1)S(1)}, u32[]{:S(2)}, u32[]{:S(2)}) collective-permute-start(bf16[64,16,128]{2,1,0:T(8,128)(2,1)S(1)} %slice_bitcast_fusion.6), channel_id=1, source_target_pairs={{0,1},{1,0},{2,3},{3,2},{4,5},{5,4},{6,7},{7,6},{8,9},{9,8},{10,11... | collective-permute-start | bytes 786440 | tf_op jit(solution)/shard_map/ppermute | solution.py:194
  95.9 35.6 %collective-permute-start.21 = (bf16[192,16,128]{2,1,0:T(8,128)(2,1)S(1)}, bf16[192,16,128]{2,1,0:T(8,128)(2,1)}, u32[]{:S(2)}, u32[]{:S(2)}) collective-permute-start(bf16[192,16,128]{2,1,0:T(8,128)(2,1)S(1)} %pad_maximum_fusion.2.refs_2_), channel_id=1, source_target_pairs={{0,8},{8,16},{16,24},{24,0},{1,9},{9,17},{17,25},{25,1},{2,10},{10... | collective-permute-start | bytes 2359304 | tf_op jit(solution)/shard_map/ppermute | solution.py:268
  112.8 33.7 %collective-permute-start.20 = (bf16[192,16,128]{2,1,0:T(8,128)(2,1)S(1)}, bf16[192,16,128]{2,1,0:T(8,128)(2,1)S(1)}, u32[]{:S(2)}, u32[]{:S(2)}) collective-permute-start(bf16[192,16,128]{2,1,0:T(8,128)(2,1)S(1)} %collective-permute-done.13.refs_2_), channel_id=1, source_target_pairs={{0,8},{8,16},{16,24},{24,0},{1,9},{9,17},{17,25},{25,1},{2,10},{10... | collective-permute-start | bytes 2359304 | tf_op jit(solution)/shard_map/ppermute | solution.py:268
  113.9 7.3 %collective-permute-start.19 = (bf16[64,16,128]{2,1,0:T(8,128)(2,1)S(1)}, bf16[64,16,128]{2,1,0:T(8,128)(2,1)S(1)}, u32[]{:S(2)}, u32[]{:S(2)}) collective-permute-start(bf16[64,16,128]{2,1,0:T(8,128)(2,1)S(1)} %slice_bitcast_fusion.4), channel_id=1, source_target_pairs={{0,3},{1,2},{2,1},{3,0},{4,7},{5,6},{6,5},{7,4},{8,11},{9,10},{10,... | collective-permute-start | bytes 786440 | tf_op jit(solution)/shard_map/ppermute | solution.py:194
  131.6 34.8 %collective-permute-start.23 = (bf16[192,16,128]{2,1,0:T(8,128)(2,1)}, bf16[192,16,128]{2,1,0:T(8,128)(2,1)}, u32[]{:S(2)}, u32[]{:S(2)}) collective-permute-start(bf16[192,16,128]{2,1,0:T(8,128)(2,1)} %collective-permute-done.21.refs_2_), channel_id=1, source_target_pairs={{0,8},{8,16},{16,24},{24,0},{1,9},{9,17},{17,25},{25,1},{2,10},{10... | collective-permute-start | bytes 2359304 | tf_op jit(solution)/shard_map/ppermute | solution.py:268
  147.4 32.9 %collective-permute-start.22 = (bf16[192,16,128]{2,1,0:T(8,128)(2,1)}, bf16[192,16,128]{2,1,0:T(8,128)(2,1)}, u32[]{:S(2)}, u32[]{:S(2)}) collective-permute-start(bf16[192,16,128]{2,1,0:T(8,128)(2,1)} %constant_dynamic-update-slice_fusion.refs_2_), channel_id=1, source_target_pairs={{0,8},{8,16},{16,24},{24,0},{1,9},{9,17},{17,25},{25,1},{2,10},{10... | collective-permute-start | bytes 2359304 | tf_op jit(solution)/shard_map/ppermute | solution.py:268
  166.4 30.8 %collective-permute-start.25 = (bf16[192,16,128]{2,1,0:T(8,128)(2,1)}, bf16[192,16,128]{2,1,0:T(8,128)(2,1)}, u32[]{:S(2)}, u32[]{:S(2)}) collective-permute-start(bf16[192,16,128]{2,1,0:T(8,128)(2,1)} %collective-permute-done.23.refs_2_), channel_id=1, source_target_pairs={{0,8},{8,16},{16,24},{24,0},{1,9},{9,17},{17,25},{25,1},{2,10},{10... | collective-permute-start | bytes 2359304 | tf_op jit(solution)/shard_map/ppermute | solution.py:268
  176.8 32.9 %copy-start.8 = (bf16[1024,1024]{1,0:T(8,128)(2,1)S(1)}, bf16[1024,1024]{1,0:T(8,128)(2,1)}, u32[]{:S(2)}) copy-start(bf16[1024,1024]{1,0:T(8,128)(2,1)} %constant.85.clone.refs_7_) | copy-start | bytes 6291460
  176.8 32.9 %copy-start.15 = (bf16[4,256,384]{2,1,0:T(8,128)(2,1)S(1)}, bf16[4,256,384]{2,1,0:T(8,128)(2,1)}, u32[]{:S(2)}) copy-start(bf16[4,256,384]{2,1,0:T(8,128)(2,1)} %get-tuple-element.105.refs_4_) | copy-start | bytes 2359300
  176.8 32.9 %copy-start.20 = (bf16[3,64,16,128]{3,2,1,0:T(8,128)(2,1)S(1)}, bf16[3,64,16,128]{3,2,1,0:T(8,128)(2,1)}, u32[]{:S(2)}) copy-start(bf16[3,64,16,128]{3,2,1,0:T(8,128)(2,1)} %copy-done.18) | copy-start | bytes 2359300
  180.3 29.4 %copy-start.4 = (f32[1024,1024]{1,0:T(8,128)S(1)}, f32[1024,1024]{1,0:T(8,128)}, u32[]{:S(2)}) copy-start(f32[1024,1024]{1,0:T(8,128)} %copy-done.3) | copy-start | bytes 12582916
  180.3 29.4 %collective-permute-start.24 = (bf16[192,16,128]{2,1,0:T(8,128)(2,1)}, bf16[192,16,128]{2,1,0:T(8,128)(2,1)}, u32[]{:S(2)}, u32[]{:S(2)}) collective-permute-start(bf16[192,16,128]{2,1,0:T(8,128)(2,1)} %collective-permute-done.22.refs_2_), channel_id=1, source_target_pairs={{0,8},{8,16},{16,24},{24,0},{1,9},{9,17},{17,25},{25,1},{2,10},{10... | collective-permute-start | bytes 2359304 | tf_op jit(solution)/shard_map/ppermute | solution.py:268
  224.9 17.3 %collective-permute-start.26 = (bf16[192,16,128]{2,1,0:T(8,128)(2,1)}, bf16[192,16,128]{2,1,0:T(8,128)(2,1)S(1)}, u32[]{:S(2)}, u32[]{:S(2)}) collective-permute-start(bf16[192,16,128]{2,1,0:T(8,128)(2,1)} %collective-permute-done.24.refs_2_), channel_id=1, source_target_pairs={{0,8},{8,16},{16,24},{24,0},{1,9},{9,17},{17,25},{25,1},{2,10},{10... | collective-permute-start | bytes 2359304 | tf_op jit(solution)/shard_map/ppermute | solution.py:268
  (20 other events, 215.3 us)
